TPU v7x, 128 devices: a whole 4x4x4 slice. The times are simulated.
128 devices in a mesh: section: 16 (over x, z_lo, core), tensor: 8 (over y, z_hi).
Axes of the slice: x: 4, y: 4, z: 4 (z_hi: 2, z_lo: 2; z = z_hi * 2 + z_lo), core: 2. Of those that a mesh axis runs over, the one named last changes fastest.
Arguments:
- query_in: bfloat16 [4096, 6144], P('section', 'tensor'), may hold values from -5 to 5
- key_in: bfloat16 [4096, 6144], P('section', 'tensor'), may hold values from -5 to 5
- value_in: bfloat16 [4096, 6144], P('section', 'tensor'), may hold values from -6 to 6
- out_grad: bfloat16 [4096, 6144], P('section', 'tensor'), may hold values from -40 to 40
- group_len: int32 [64], replicated, may hold values from 1 to 64, 3072 in all
Outputs:
- attn_out: bfloat16 [4096, 6144], P(('section', 'tensor'))
- query_grad: bfloat16 [4096, 6144], P(('section', 'tensor'))
- key_grad: bfloat16 [4096, 6144], P(('section', 'tensor'))
- value_grad: bfloat16 [4096, 6144], P(('section', 'tensor'))
Inputs may be any that keep to these rules, and one draw needn't show every extreme that they name: Group c holds the tokens at positions c * 64 to c * 64 + group_len[c] - 1; the other slots of its 64 are padding; the lengths sum to 3072.
All inputs are finite; a program needn't handle non-finite values.
Results may differ from a plain program's by a relative error of at most 0.035.
Values may be sent and summed in bfloat16 or wider, within the bound.
A program may use at most 128 MiB of HBM per device.

v0:
```python
import math

import jax
import jax.numpy as jnp
from jax import lax
from jax.sharding import PartitionSpec as P

HSIZE = 128
CSLOT = 64


NEG_FILL = -1e30


def block_plan(total_rows):
    block_rows = math.gcd(total_rows, 512)
    return (block_rows, total_rows // block_rows)


def per_device(query_in, key_in, value_in, out_grad, group_len):
    rows_dev = query_in.shape[0]
    head_count = query_in.shape[1] // HSIZE
    seq_len = rows_dev * lax.axis_size("section")
    score_scale = 1.0 / math.sqrt(HSIZE)
    first_row = lax.axis_index("section") * rows_dev
    positions = jnp.arange(seq_len, dtype=jnp.int32)
    slot_lens = jnp.repeat(group_len, CSLOT, total_repeat_length=seq_len)
    is_valid = positions % CSLOT < slot_lens
    my_rows = first_row + jnp.arange(rows_dev, dtype=jnp.int32)
    my_valid = lax.dynamic_slice_in_dim(is_valid, first_row, rows_dev)
    row_keep = my_valid.astype(jnp.float32)[:, None, None]
    query_heads = query_in.reshape(rows_dev, head_count, HSIZE)
    key_heads = key_in.reshape(rows_dev, head_count, HSIZE)
    value_heads = value_in.reshape(rows_dev, head_count, HSIZE)
    grad_heads = (
        out_grad.reshape(rows_dev, head_count, HSIZE).astype(jnp.float32) * row_keep
    ).astype(jnp.bfloat16)
    grad_loc = grad_heads.reshape(rows_dev, head_count * HSIZE)
    row_init = jnp.full((rows_dev, head_count), NEG_FILL, jnp.float32)
    zero_rows = jnp.zeros((rows_dev, head_count), jnp.float32)
    zero_acc = jnp.zeros((rows_dev, head_count, HSIZE), jnp.float32)

    def key_block(shard_part, offset, block_rows):
        key_part, value_part = shard_part
        key_block_h = lax.dynamic_slice_in_dim(key_part, offset, block_rows).reshape(
            block_rows, head_count, HSIZE
        )
        value_block_h = lax.dynamic_slice_in_dim(value_part, offset, block_rows).reshape(
            block_rows, head_count, HSIZE
        )
        key_rows = offset + jnp.arange(block_rows, dtype=jnp.int32)
        key_valid = lax.dynamic_slice_in_dim(is_valid, offset, block_rows)
        allowed = ((key_rows[None, :] <= my_rows[:, None]) & key_valid[None, :])[:, None, :]
        scores = (
            jnp.einsum("qhd,khd->qhk", query_heads, key_block_h, preferred_element_type=jnp.float32)
            * score_scale
        )
        return (key_block_h, value_block_h, allowed, jnp.where(allowed, scores, NEG_FILL))

    def online_update(row_top, row_total, scores, allowed):
        new_top = jnp.maximum(row_top, jnp.max(scores, axis=2))
        factor = jnp.exp(row_top - new_top)
        weights = jnp.where(allowed, jnp.exp(scores - new_top[:, :, None]), 0.0)
        return (new_top, row_total * factor + jnp.sum(weights, axis=2), factor[:, :, None], weights)

    running = (row_init, zero_rows, zero_acc)
    shard_part = (
        lax.all_gather(key_in, "section", axis=0, tiled=True),
        lax.all_gather(value_in, "section", axis=0, tiled=True),
    )
    block_rows, block_count = block_plan(shard_part[0].shape[0])

    def forward_block_step(state_now, block_index):
        row_top, row_total, out_acc = state_now
        key_block_h, value_block_h, allowed, scores = key_block(
            shard_part, block_index * block_rows, block_rows
        )
        new_top, new_total, rescale, weights = online_update(row_top, row_total, scores, allowed)
        out_acc = out_acc * rescale + jnp.einsum(
            "qhk,khd->qhd",
            weights.astype(jnp.bfloat16),
            value_block_h,
            preferred_element_type=jnp.float32,
        )
        return ((new_top, new_total, out_acc), None)

    running, _ = lax.scan(forward_block_step, running, jnp.arange(block_count))
    row_top, row_total, out_acc = running
    out_full = out_acc / row_total[:, :, None]
    row_delta = jnp.sum(grad_heads.astype(jnp.float32) * out_full, axis=2)
    log_total = row_top + jnp.log(row_total)
    running = zero_acc
    grad_shard_part = (
        lax.all_gather(key_in, "section", axis=0, tiled=True),
        lax.all_gather(value_in, "section", axis=0, tiled=True),
    )
    grad_block_rows, block_count = block_plan(grad_shard_part[0].shape[0])

    def grad_block_step(query_sum, block_index):
        key_block_h, value_block_h, allowed, scores = key_block(
            grad_shard_part, block_index * grad_block_rows, grad_block_rows
        )
        weights = jnp.where(allowed, jnp.exp(scores - log_total[:, :, None]), 0.0)
        grad_scores = jnp.einsum(
            "qhd,khd->qhk", grad_heads, value_block_h, preferred_element_type=jnp.float32
        )
        score_grad = (weights * (grad_scores - row_delta[:, :, None]) * score_scale).astype(
            jnp.bfloat16
        )
        query_sum = query_sum + jnp.einsum(
            "qhk,khd->qhd", score_grad, key_block_h, preferred_element_type=jnp.float32
        )
        return (query_sum, None)

    running, _ = lax.scan(grad_block_step, running, jnp.arange(block_count))
    query_acc = running
    log_all, delta_all = (
        lax.all_gather(log_total, "section", axis=0, tiled=True),
        lax.all_gather(row_delta, "section", axis=0, tiled=True),
    )
    running = (zero_acc, zero_acc)
    query_part = lax.all_gather(query_in, "section", axis=0, tiled=True)
    grad_part = lax.all_gather(grad_loc, "section", axis=0, tiled=True)
    key_block_rows, block_count = block_plan(query_part.shape[0])

    def key_block_step(state_now, block_index):
        key_acc, value_acc = state_now
        offset = block_index * key_block_rows
        query_block_h = lax.dynamic_slice_in_dim(query_part, offset, key_block_rows).reshape(
            key_block_rows, head_count, HSIZE
        )
        grad_block_h = lax.dynamic_slice_in_dim(grad_part, offset, key_block_rows).reshape(
            key_block_rows, head_count, HSIZE
        )
        log_block = lax.dynamic_slice_in_dim(log_all, offset, key_block_rows)
        delta_block = lax.dynamic_slice_in_dim(delta_all, offset, key_block_rows)
        query_rows = offset + jnp.arange(key_block_rows, dtype=jnp.int32)
        allowed = ((my_rows[None, :] <= query_rows[:, None]) & my_valid[None, :])[:, None, :]
        scores = (
            jnp.einsum("qhd,khd->qhk", query_block_h, key_heads, preferred_element_type=jnp.float32)
            * score_scale
        )
        weights = jnp.where(allowed, jnp.exp(scores - log_block[:, :, None]), 0.0)
        grad_scores = jnp.einsum(
            "qhd,khd->qhk", grad_block_h, value_heads, preferred_element_type=jnp.float32
        )
        score_grad = (weights * (grad_scores - delta_block[:, :, None]) * score_scale).astype(
            jnp.bfloat16
        )
        value_acc = value_acc + jnp.einsum(
            "qhk,qhd->khd",
            weights.astype(jnp.bfloat16),
            grad_block_h,
            preferred_element_type=jnp.float32,
        )
        key_acc = key_acc + jnp.einsum(
            "qhk,qhd->khd", score_grad, query_block_h, preferred_element_type=jnp.float32
        )
        return ((key_acc, value_acc), None)

    running, _ = lax.scan(key_block_step, running, jnp.arange(block_count))
    key_acc, value_acc = running
    flat_shape = (rows_dev, head_count * HSIZE)
    attn_loc = (out_full * row_keep).reshape(flat_shape).astype(jnp.bfloat16)
    query_flat = query_acc.reshape(flat_shape).astype(jnp.bfloat16)
    key_flat = key_acc.reshape(flat_shape).astype(jnp.bfloat16)
    value_flat = value_acc.reshape(flat_shape).astype(jnp.bfloat16)
    return (
        lax.all_to_all(attn_loc, "tensor", split_axis=0, concat_axis=1, tiled=True),
        lax.all_to_all(query_flat, "tensor", split_axis=0, concat_axis=1, tiled=True),
        lax.all_to_all(key_flat, "tensor", split_axis=0, concat_axis=1, tiled=True),
        lax.all_to_all(value_flat, "tensor", split_axis=0, concat_axis=1, tiled=True),
    )


def solution(mesh):
    in_specs = (
        P("section", "tensor"),
        P("section", "tensor"),
        P("section", "tensor"),
        P("section", "tensor"),
        P(),
    )
    out_specs = (
        P(("section", "tensor"), None),
        P(("section", "tensor"), None),
        P(("section", "tensor"), None),
        P(("section", "tensor"), None),
    )
    return jax.shard_map(
        per_device, mesh=mesh, in_specs=in_specs, out_specs=out_specs, check_vma=False
    )
```

profile of v0, /device:TPU:1, one launch (start us, length us, event | category | flops | bytes accessed | tf_op | source)
XLA Modules:
  0.0 515.2 jit_solution(4525082624836803256)
XLA Ops:
  16.5 4.4 compare_select_fusion.1
  23.9 36.4 %fusion.59 = pred[4096]{0:T(1024)(128)(4,1)} fusion(pred[4096]{0:T(1024)(128)(4,1)S(1)} %get-tuple-element.478, pred[4096]{0:T(1024)(128)(4,1)S(1)} %get-tuple-element.477, pred[4096]{0:T(1024)(128)(4,1)S(1)} %get-tuple-element.476, pred[4096]{0:T(1024)(128)(4,1)S(1)} %get-tuple-element.475, pred[4096]{0:T(1024)(128)(4,1)S(1)} %get-tuple-element.474, ...), kind=kLoop, calls=%fused_computation.146 | loop fusion | flops 299008 | bytes 270692 | tf_op jit(solution)/shard_map/lt | solution.py:28
  66.0 54.9 %all-gather.7.cloned.1.call-done = bf16[4096,768]{0,1:T(8,128)(2,1)} async-done(((bf16[256,768]{0,1:T(8,128)(2,1)}), bf16[4096,768]{0,1:T(8,128)(2,1)}) %all-gather.7.cloned.1.call-update) | async-done | bytes 6291472 | tf_op jit(solution)/shard_map/all_gather | solution.py:69
  121.4 80.0 %while.40 = (s32[]{:T(128)}, f32[256,6]{0,1:T(8,128)S(1)}, f32[256,6]{0,1:T(8,128)}, f32[256,6,128]{0,2,1:T(8,128)}, s32[8]{0:T(128)}, /*index=5*/pred[4096]{0:T...) while((s32[]{:T(128)}, f32[256,6]{0,1:T(8,128)S(1)}, ...), condition=%wide.region_3.4_spmd.clone, body=%wide.region_0.3_spmd.clone.sunk | while | flops 413737216 | bytes 27287460 | solution.py:87
  204.4 6.5 %all-to-all-start = ((bf16[8,32,768]{2,1,0:T(8,128)(2,1)}), bf16[8,32,768]{2,1,0:T(8,128)(2,1)}, u32[]{:S(2)}, u32[]{:S(2)}) async-start(bf16[8,32,768]{2,1,0:T(8,128)(2,1)} %convert_element_type.63), calls=%async_computation | async-start | bytes 786432 | tf_op jit(solution)/shard_map/all_to_all | solution.py:169
  213.1 93.8 %while.41 = (s32[]{:T(128)}, f32[256,6,128]{0,2,1:T(8,128)}, s32[8]{0:T(128)}, bf16[4096,768]{0,1:T(8,128)(2,1)}, pred[4096]{0:T(1024)(128)(4,1)}, /*index=5*/bf...) while((s32[]{:T(128)}, f32[256,6,128]{0,2,1:T(8,128)}, ...), condition=%wide.region_6.7_spmd.clone, body=%wide.region_5.6_spmd.clone.sunk | while | flops 610927360 | bytes 17608480 | solution.py:115
  220.5 4.1 fusion.123
  231.9 4.3 fusion.123
  243.7 4.3 fusion.123
  255.4 4.3 fusion.123
  267.2 4.3 fusion.123
  279.0 4.3 fusion.123
  290.8 4.3 fusion.123
  302.6 4.3 fusion.123
  309.7 19.3 %all_gather.23 = f32[4096,6]{0,1:T(8,128)} all-gather(f32[256,6]{0,1:T(8,128)} %get-tuple-element.1012), channel_id=1, replica_groups=mesh['section'=16,'tensor'=8] {'section'}, dimensions={0}, use_global_device_ids=true | all-gather | bytes 104448 | tf_op jit(solution)/shard_map/all_gather | solution.py:118
  329.0 18.6 %all_gather.25 = f32[4096,6]{0,1:T(8,128)} all-gather(f32[256,6]{0,1:T(8,128)S(1)} %get-tuple-element.1011), channel_id=1, replica_groups=mesh['section'=16,'tensor'=8] {'section'}, dimensions={0}, use_global_device_ids=true | all-gather | bytes 104448 | tf_op jit(solution)/shard_map/all_gather | solution.py:119
  347.6 7.0 %all-to-all-start.1 = ((bf16[8,32,768]{2,1,0:T(8,128)(2,1)}), bf16[8,32,768]{2,1,0:T(8,128)(2,1)}, u32[]{:S(2)}, u32[]{:S(2)}) async-start(bf16[8,32,768]{2,1,0:T(8,128)(2,1)} %convert_element_type.69), calls=%async_computation.1 | async-start | bytes 786432 | tf_op jit(solution)/shard_map/all_to_all | solution.py:170
  355.1 123.0 %while.42 = (s32[]{:T(128)}, f32[256,6,128]{0,2,1:T(8,128)}, f32[256,6,128]{0,2,1:T(8,128)}, s32[8]{0:T(128)}, bf16[4096,768]{0,1:T(8,128)(2,1)}, /*index=5*/pre...) while((s32[]{:T(128)}, f32[256,6,128]{0,2,1:T(8,128)}, ...), condition=%wide.region_8.9_spmd.clone, body=%wide.region_7.8_spmd.clone.sunk | while | flops 815006464 | bytes 23293480 | solution.py:161
  363.0 4.1 fusion.132
  378.0 4.3 fusion.132
  393.4 4.3 fusion.132
  397.7 3.2 fusion.133
  408.9 4.3 fusion.132
  424.3 4.3 fusion.132
  428.6 3.2 fusion.133
  439.7 4.3 fusion.132
  455.2 4.3 fusion.132
  470.6 4.3 fusion.132
  480.9 6.6 %all-to-all-start.2 = ((bf16[8,32,768]{2,1,0:T(8,128)(2,1)}), bf16[8,32,768]{2,1,0:T(8,128)(2,1)S(1)}, u32[]{:S(2)}, u32[]{:S(2)}) async-start(bf16[8,32,768]{2,1,0:T(8,128)(2,1)} %convert_element_type.73), calls=%async_computation.2 | async-start | bytes 786432 | tf_op jit(solution)/shard_map/all_to_all | solution.py:171
  489.2 6.3 %all-to-all-done.2 = bf16[8,32,768]{2,1,0:T(8,128)(2,1)S(1)} async-done(((bf16[8,32,768]{2,1,0:T(8,128)(2,1)}), bf16[8,32,768]{2,1,0:T(8,128)(2,1)S(1)}, u32[]{:S(2)}, u32[]{:S(2)}) %all-to-all-start.2) | async-done | bytes 393248 | tf_op jit(solution)/shard_map/all_to_all | solution.py:171
  495.4 4.6 all-to-all-start.3
  504.4 3.5 all-to-all-done.3
  (468 shorter events, 240.3 us)
Async XLA Ops:
  7.2 9.3 %copy-start.18 = (s32[32,128]{1,0:T(8,128)S(1)}, s32[32,128]{1,0:T(8,128)}, u32[]{:S(2)}) copy-start(s32[32,128]{1,0:T(8,128)} %constant.161.clone.1) | copy-start | bytes 49156
  7.2 6.2 %copy-start.17 = (bf16[256,768]{1,0:T(8,128)(2,1)S(1)}, bf16[256,768]{1,0:T(8,128)(2,1)}, u32[]{:S(2)}) copy-start(bf16[256,768]{1,0:T(8,128)(2,1)} %param.16) | copy-start | bytes 1179652
  7.2 6.4 %copy-start.10 = (s32[64]{0:T(128)S(1)}, s32[64]{0:T(128)}, u32[]{:S(2)}) copy-start(s32[64]{0:T(128)} %param.17) | copy-start | bytes 772
  7.2 58.8 %all-gather.5.cloned.1.call-start = ((), (), s32[]{:S(2)}) async-start(), calls=%async_computation.4 | async-start | bytes 6684672 | tf_op jit(solution)/shard_map/all_gather | solution.py:68
  9.2 54.0 %copy-start.8 = (bf16[256,768]{0,1:T(8,128)(2,1)S(1)}, bf16[256,768]{0,1:T(8,128)(2,1)}, u32[]{:S(2)}) copy-start(bf16[256,768]{0,1:T(8,128)(2,1)} %copy.77) | copy-start | bytes 1179652
  9.2 111.7 %all-gather.7.cloned.1.call-start = ((), (), s32[]{:S(2)}) async-start(), calls=%async_computation.5 | async-start | bytes 6684672 | tf_op jit(solution)/shard_map/all_gather | solution.py:69
  11.2 52.9 %copy-start.9 = (bf16[256,768]{0,1:T(8,128)(2,1)S(1)}, bf16[256,768]{0,1:T(8,128)(2,1)}, u32[]{:S(2)}) copy-start(bf16[256,768]{0,1:T(8,128)(2,1)} %copy.79) | copy-start | bytes 1179652
  11.3 343.3 %all-gather.9.cloned.1.call-start = ((), (), s32[]{:S(2)}) async-start(), calls=%async_computation.6 | async-start | bytes 6684672 | tf_op jit(solution)/shard_map/all_gather | solution.py:122
  13.3 49.7 %copy-start.7 = (bf16[256,768]{0,1:T(8,128)(2,1)S(1)}, bf16[256,768]{0,1:T(8,128)(2,1)}, u32[]{:S(2)}) copy-start(bf16[256,768]{0,1:T(8,128)(2,1)} %copy.78) | copy-start | bytes 1179652
  13.3 341.3 %all-gather.11.cloned.1.call-start = ((), (), s32[]{:S(2)}) async-start(), calls=%async_computation.7 | async-start | bytes 6684672 | tf_op jit(solution)/shard_map/all_gather | solution.py:123
  13.5 49.5 %copy-start.6 = (bf16[256,768]{0,1:T(8,128)(2,1)}, bf16[256,768]{0,1:T(8,128)(2,1)S(1)}, u32[]{:S(2)}) copy-start(bf16[256,768]{0,1:T(8,128)(2,1)S(1)} %copy.83) | copy-start | bytes 1179652
  201.4 9.6 %copy-start.16 = (f32[256,6]{0,1:T(8,128)S(1)}, f32[256,6]{0,1:T(8,128)}, u32[]{:S(2)}) copy-start(f32[256,6]{0,1:T(8,128)} %get-tuple-element.191) | copy-start | bytes 18436
  204.4 143.1 %all-to-all-start = ((bf16[8,32,768]{2,1,0:T(8,128)(2,1)}), bf16[8,32,768]{2,1,0:T(8,128)(2,1)}, u32[]{:S(2)}, u32[]{:S(2)}) async-start(bf16[8,32,768]{2,1,0:T(8,128)(2,1)} %convert_element_type.63), calls=%async_computation | async-start | bytes 786432 | tf_op jit(solution)/shard_map/all_to_all | solution.py:169
  215.0 5.5 %copy-start.19 = (f32[256,6]{0,1:T(8,128)S(1)}, f32[256,6]{0,1:T(8,128)}, u32[]{:S(2)}) copy-start(f32[256,6]{0,1:T(8,128)} %get-tuple-element.933) | copy-start | bytes 18436 | tf_op jit(solution)/shard_map/while
  226.4 5.5 %copy-start.19 = (f32[256,6]{0,1:T(8,128)S(1)}, f32[256,6]{0,1:T(8,128)}, u32[]{:S(2)}) copy-start(f32[256,6]{0,1:T(8,128)} %get-tuple-element.933) | copy-start | bytes 18436 | tf_op jit(solution)/shard_map/while
  238.2 5.5 %copy-start.19 = (f32[256,6]{0,1:T(8,128)S(1)}, f32[256,6]{0,1:T(8,128)}, u32[]{:S(2)}) copy-start(f32[256,6]{0,1:T(8,128)} %get-tuple-element.933) | copy-start | bytes 18436 | tf_op jit(solution)/shard_map/while
  249.9 5.5 %copy-start.19 = (f32[256,6]{0,1:T(8,128)S(1)}, f32[256,6]{0,1:T(8,128)}, u32[]{:S(2)}) copy-start(f32[256,6]{0,1:T(8,128)} %get-tuple-element.933) | copy-start | bytes 18436 | tf_op jit(solution)/shard_map/while
  261.7 5.5 %copy-start.19 = (f32[256,6]{0,1:T(8,128)S(1)}, f32[256,6]{0,1:T(8,128)}, u32[]{:S(2)}) copy-start(f32[256,6]{0,1:T(8,128)} %get-tuple-element.933) | copy-start | bytes 18436 | tf_op jit(solution)/shard_map/while
  273.5 5.5 %copy-start.19 = (f32[256,6]{0,1:T(8,128)S(1)}, f32[256,6]{0,1:T(8,128)}, u32[]{:S(2)}) copy-start(f32[256,6]{0,1:T(8,128)} %get-tuple-element.933) | copy-start | bytes 18436 | tf_op jit(solution)/shard_map/while
  285.2 5.5 %copy-start.19 = (f32[256,6]{0,1:T(8,128)S(1)}, f32[256,6]{0,1:T(8,128)}, u32[]{:S(2)}) copy-start(f32[256,6]{0,1:T(8,128)} %get-tuple-element.933) | copy-start | bytes 18436 | tf_op jit(solution)/shard_map/while
  297.0 5.5 %copy-start.19 = (f32[256,6]{0,1:T(8,128)S(1)}, f32[256,6]{0,1:T(8,128)}, u32[]{:S(2)}) copy-start(f32[256,6]{0,1:T(8,128)} %get-tuple-element.933) | copy-start | bytes 18436 | tf_op jit(solution)/shard_map/while
  306.9 48.2 %copy-start.5 = (bf16[256,6,128]{2,0,1:T(8,128)(2,1)S(1)}, bf16[256,6,128]{2,0,1:T(8,128)(2,1)}, u32[]{:S(2)}) copy-start(bf16[256,6,128]{2,0,1:T(8,128)(2,1)} %copy.91) | copy-start | bytes 1179652
  347.6 133.4 %all-to-all-start.1 = ((bf16[8,32,768]{2,1,0:T(8,128)(2,1)}), bf16[8,32,768]{2,1,0:T(8,128)(2,1)}, u32[]{:S(2)}, u32[]{:S(2)}) async-start(bf16[8,32,768]{2,1,0:T(8,128)(2,1)} %convert_element_type.69), calls=%async_computation.1 | async-start | bytes 786432 | tf_op jit(solution)/shard_map/all_to_all | solution.py:170
  371.9 5.2 %copy-start.20 = (pred[256]{0:T(512)(128)(4,1)S(1)}, pred[256]{0:T(512)(128)(4,1)}, u32[]{:S(2)}) copy-start(pred[256]{0:T(512)(128)(4,1)} %get-tuple-element.979) | copy-start | bytes 772 | tf_op jit(solution)/shard_map/while
  387.3 5.2 %copy-start.20 = (pred[256]{0:T(512)(128)(4,1)S(1)}, pred[256]{0:T(512)(128)(4,1)}, u32[]{:S(2)}) copy-start(pred[256]{0:T(512)(128)(4,1)} %get-tuple-element.979) | copy-start | bytes 772 | tf_op jit(solution)/shard_map/while
  402.8 5.2 %copy-start.20 = (pred[256]{0:T(512)(128)(4,1)S(1)}, pred[256]{0:T(512)(128)(4,1)}, u32[]{:S(2)}) copy-start(pred[256]{0:T(512)(128)(4,1)} %get-tuple-element.979) | copy-start | bytes 772 | tf_op jit(solution)/shard_map/while
  418.2 5.2 %copy-start.20 = (pred[256]{0:T(512)(128)(4,1)S(1)}, pred[256]{0:T(512)(128)(4,1)}, u32[]{:S(2)}) copy-start(pred[256]{0:T(512)(128)(4,1)} %get-tuple-element.979) | copy-start | bytes 772 | tf_op jit(solution)/shard_map/while
  433.7 5.2 %copy-start.20 = (pred[256]{0:T(512)(128)(4,1)S(1)}, pred[256]{0:T(512)(128)(4,1)}, u32[]{:S(2)}) copy-start(pred[256]{0:T(512)(128)(4,1)} %get-tuple-element.979) | copy-start | bytes 772 | tf_op jit(solution)/shard_map/while
  464.6 5.2 %copy-start.20 = (pred[256]{0:T(512)(128)(4,1)S(1)}, pred[256]{0:T(512)(128)(4,1)}, u32[]{:S(2)}) copy-start(pred[256]{0:T(512)(128)(4,1)} %get-tuple-element.979) | copy-start | bytes 772 | tf_op jit(solution)/shard_map/while
  478.1 9.4 %copy-start.13 = (f32[256,6,128]{0,2,1:T(8,128)S(1)}, f32[256,6,128]{0,2,1:T(8,128)}, u32[]{:S(2)}) copy-start(f32[256,6,128]{0,2,1:T(8,128)} %get-tuple-element.195) | copy-start | bytes 2359300
  480.9 14.5 %all-to-all-start.2 = ((bf16[8,32,768]{2,1,0:T(8,128)(2,1)}), bf16[8,32,768]{2,1,0:T(8,128)(2,1)S(1)}, u32[]{:S(2)}, u32[]{:S(2)}) async-start(bf16[8,32,768]{2,1,0:T(8,128)(2,1)} %convert_element_type.73), calls=%async_computation.2 | async-start | bytes 786432 | tf_op jit(solution)/shard_map/all_to_all | solution.py:171
  495.4 12.4 %all-to-all-start.3 = ((bf16[8,32,768]{2,1,0:T(8,128)(2,1)}), bf16[8,32,768]{2,1,0:T(8,128)(2,1)S(1)}, u32[]{:S(2)}, u32[]{:S(2)}) async-start(bf16[8,32,768]{2,1,0:T(8,128)(2,1)} %convert_element_type.75), calls=%async_computation.3 | async-start | bytes 786432 | tf_op jit(solution)/shard_map/all_to_all | solution.py:172
  (75 other events, 127.3 us)
Sparse Core Ops, SparseCore 0:
  10.2 55.7 all-gather.4
  68.2 52.6 all-gather.6
  123.1 52.3 all-gather.8
  177.0 58.3 all-gather.10
where the time goes:
time: 521 us; the launch traced here: 515 us
  local copies, waits for them, and re-layouts  156 us (30%)
  matrix products  119 us (23%)
  other arithmetic  80.2 us (15%)
  waiting for transfers between devices  65.7 us (13%)
  blocking collectives  37.9 us (7%)
  starting transfers between devices  24.9 us (5%)
  loops' own time  17.5 us (3%)
  between operations  14 us (3%)
    all_gather x1, waiting for transfers between devices, per_device(): lax.all_gather(value_in, 'section', axis=0, tiled=True)  54.9 us
    dynamic_slice x16, local copies, waits for them, and re-layouts, key_block(): lax.dynamic_slice_in_dim(value_part, offset, block_rows)  38.4 us
    lt x1, other arithmetic, per_device(): is_valid = positions % CSLOT < slot_lens  36.4 us
    dot_general x8, matrix products, grad_block_step(): jnp.einsum('qhk,khd->qhd', score_grad, key_block_h, preferred_element_typ...  34.5 us
    dot_general x8, matrix products, key_block_step(): jnp.einsum('qhk,qhd->khd', score_grad, query_block_h, preferred_element_t...  34.4 us
    dynamic_slice x24, local copies, waits for them, and re-layouts, per_device(): running, _ = lax.scan(forward_block_step, running, jnp.arange(block_count))  29.8 us
    dot_general x8, matrix products, key_block_step(): jnp.einsum('qhk,qhd->khd', weights.astype(jnp.bfloat16), grad_block_h, pr...  25 us
    while x184, local copies, waits for them, and re-layouts  21.4 us
  transfers between devices with their start and end apart: 8, of which 4 were waited for; matrix products, arithmetic and copies ran while one was open for 64% of the time, Pallas kernels for 0%

commit v1 on v0

v1 whole, which is shorter than its diff:
```python
import functools
import math

import jax
import jax.numpy as jnp
from jax import lax
from jax.experimental import pallas as pl
from jax.experimental.pallas import tpu as pltpu
from jax.sharding import PartitionSpec as P

HSIZE = 128
CSLOT = 64
NEG_FILL = -1e30
MESH = pl.DeviceIdType.MESH
F32 = jnp.float32
BF16 = jnp.bfloat16


def chip_of(head, tensor, chips):
    if chips != 8:
        return lax.rem(head + tensor, chips)
    level = head // 3
    x = lax.rem(lax.rem(head, 3) + 2 * level + tensor // 2, 4)
    return 2 * x + level


def head_at(chip, tensor, chips, heads):
    if chips != 8:
        head = lax.rem(chip - lax.rem(tensor, chips) + chips, chips)
        return (head, head < heads)
    level = lax.rem(chip, 2)
    place = lax.rem(chip // 2 + 8 - 2 * level - tensor // 2, 4)
    return (3 * level + place, place < 3)


def dot(a, b, dims):
    return lax.dot_general(a, b, ((dims[:1], dims[1:]), ((), ())), preferred_element_type=F32)


def attention_kernel(
    sections, tensors, heads,
    len_ref, q_ref, k_ref, v_ref, g_ref, out_ref,
    kbuf, vbuf, qbuf, gbuf, kt, vt, bias, ones, sbuf, pbuf, outt, totals, dqt, dk, dv,
    stage, xsend, xrecv,
    recv_sem, fwd_sem, send_sem, fsend_sem, xsend_sem, xrecv_sem, osend_sem, orecv_sem,
):
    rows = q_ref.shape[0]
    half_rows = rows // 2
    chunk = rows // tensors
    half_tensors = tensors // 2
    chips = sections // 2
    blocks = sections // 2
    key_rows = 2 * rows
    score_scale = 1.0 / math.sqrt(HSIZE)
    exp_scale = score_scale * math.log2(math.e)

    me_s = lax.axis_index("section")
    me_t = lax.axis_index("tensor")
    core = lax.rem(me_s, 2)
    sibling = me_s + 1 - 2 * core
    head, active = head_at(me_s // 2, me_t, chips, heads)
    inputs = (k_ref, q_ref, v_ref, g_ref)
    landing = (kbuf, qbuf, vbuf, gbuf)

    def aligned(start, size, step):
        return pl.ds(pl.multiple_of(start, step), size)

    def half_of(section, of_core):
        return lax.rem(of_core + section, 2)

    def key_rows_of(section, half):
        return aligned(section * rows + half * half_rows, half_rows, half_rows)

    def own_rows_of(section):
        return aligned(section * half_rows, half_rows, half_rows)

    def slot(kind, section, half):
        return landing[kind].at[key_rows_of(section, half) if kind in (0, 2) else own_rows_of(section)]

    barrier = pltpu.get_barrier_semaphore()

    @pl.when(active)
    def _():
        @pl.loop(1, sections)
        def _(step):
            pl.semaphore_signal(
                barrier, inc=1, device_id={"section": lax.rem(me_s + step, sections)}, device_id_type=MESH
            )

    out_core = lax.rem(core + me_t // half_tensors, 2)

    @pl.loop(0, tensors)
    def _(tensor):
        @pl.loop(0, heads)
        def _(index):
            target = 2 * chip_of(index, tensor, chips) + out_core

            @pl.when(jnp.logical_or(target != me_s, tensor != me_t))
            def _():
                pl.semaphore_signal(
                    barrier, inc=1, device_id={"section": target, "tensor": tensor}, device_id_type=MESH
                )

    to_itself = me_t < half_tensors
    is_active = active.astype(jnp.int32)
    pl.semaphore_wait(
        barrier,
        2 * heads - is_active + is_active * (sections * half_tensors - to_itself.astype(jnp.int32)),
    )

    for kind in range(4):
        @pl.loop(0, heads)
        def _(step, kind=kind):
            index = lax.rem(step + me_s // 2, heads)
            chip = chip_of(index, me_t, chips)
            for half_step in range(2):
                target_core = core if half_step == 0 else 1 - core
                target = 2 * chip + target_core
                half = half_of(me_s, target_core)
                source = inputs[kind].at[
                    aligned(half * half_rows, half_rows, half_rows), aligned(index * HSIZE, HSIZE, HSIZE)
                ]
                place = slot(kind, me_s, half)

                def send():
                    pltpu.make_async_remote_copy(
                        src_ref=source, dst_ref=place,
                        send_sem=send_sem.at[kind], recv_sem=recv_sem.at[kind, me_s],
                        device_id={"section": target}, device_id_type=MESH,
                    ).start()

                if half_step == 0:
                    @pl.when(target != me_s)
                    def _():
                        send()

                    @pl.when(target == me_s)
                    def _():
                        pltpu.make_async_copy(source, place, recv_sem.at[kind, me_s]).start()
                else:
                    send()

    def wait_arrival(kind, section):
        place = slot(kind, section, half_of(section, core))
        pltpu.make_async_copy(place, place, recv_sem.at[kind, section]).wait()

    def forward(kind):
        which = kind // 2

        @pl.loop(0, sections)
        def _(section):
            wait_arrival(kind, section)
            place = slot(kind, section, half_of(section, core))
            pltpu.make_async_remote_copy(
                src_ref=place, dst_ref=place,
                send_sem=fsend_sem.at[which], recv_sem=fwd_sem.at[which, section],
                device_id={"section": sibling}, device_id_type=MESH,
            ).start()

    def wait_forwarded(kind):
        which = kind // 2

        @pl.loop(0, sections)
        def _(section):
            place = slot(kind, section, half_of(section, 1 - core))
            pltpu.make_async_copy(place, place, fwd_sem.at[which, section]).wait()

    def group_len_of(group):
        return len_ref[group]

    @pl.when(active)
    def _():
        lane = lax.broadcasted_iota(jnp.int32, (CSLOT, HSIZE), 1)
        row = lax.broadcasted_iota(jnp.int32, (CSLOT, HSIZE), 0)

        @pl.loop(0, sections * rows // CSLOT)
        def _(group):
            padded = jnp.logical_and(row >= group_len_of(group), lane == 0)
            bias[aligned(group * CSLOT, CSLOT, CSLOT)] = jnp.where(padded, NEG_FILL, 0.0).astype(BF16)

        ones[...] = jnp.where(
            lax.broadcasted_iota(jnp.int32, ones.shape, 1) == 0, 1.0, 0.0
        ).astype(BF16)

        @pl.loop(0, blocks)
        def _(block):
            span = aligned(block * key_rows, key_rows, key_rows)
            dk[span] = jnp.zeros((key_rows, HSIZE), F32)
            dv[span] = jnp.zeros((key_rows, HSIZE), F32)

        forward(0)

        @pl.loop(0, sections)
        def _(section):
            wait_arrival(1, section)

        forward(2)
        wait_forwarded(0)
        wait_forwarded(2)

        @pl.loop(0, blocks)
        def _(block):
            span = aligned(block * key_rows, key_rows, key_rows)
            kt[:, span] = kbuf[span].T
            vt[:, span] = vbuf[span].T

        def p_span(block, index):
            return aligned((block * (block + 1) // 2 + index) * key_rows, key_rows, key_rows)

        def key_span(index):
            return aligned(index * key_rows, key_rows, key_rows)

        def own_span(block):
            return aligned(block * rows, rows, rows)

        lane_q = lax.broadcasted_iota(jnp.int32, (1, rows), 1)
        query_place = jnp.where(
            lane_q < half_rows, core * half_rows + lane_q, rows + (1 - core) * half_rows + lane_q - half_rows
        )

        @pl.loop(0, blocks)
        def _(block):
            query_wide = jnp.concatenate([qbuf[own_span(block)], ones[...]], axis=1)

            def score_step(index, top, diagonal=False):
                span = key_span(index)
                key_wide = jnp.concatenate([kbuf[span], bias[span]], axis=1)
                scores = dot(key_wide, query_wide, (1, 1))
                if diagonal:
                    place = lax.broadcasted_iota(jnp.int32, (key_rows, rows), 0)
                    scores = jnp.where(place <= query_place, scores, NEG_FILL)
                sbuf[span] = scores
                return jnp.maximum(top, jnp.max(scores.reshape(key_rows // 8, 8, rows), axis=0))

            top = lax.fori_loop(0, block, score_step, jnp.full((8, rows), NEG_FILL, F32))
            top = score_step(block, top, diagonal=True)
            shift = jnp.max(top, axis=0, keepdims=True) * exp_scale
            outt[block] = jnp.zeros((HSIZE, rows), F32)

            def weight_step(index, total):
                span = key_span(index)
                weights = jnp.exp2(sbuf[span] * exp_scale - shift)
                low = weights.astype(BF16)
                pbuf[p_span(block, index)] = low
                outt[block] += dot(vt[:, span], low, (1, 0))
                return total + jnp.sum(weights.reshape(key_rows // 8, 8, rows), axis=0)

            total = lax.fori_loop(0, block + 1, weight_step, jnp.zeros((8, rows), F32))
            totals[block] = jnp.sum(total, axis=0, keepdims=True)

        @pl.loop(0, sections)
        def _(section):
            wait_arrival(3, section)

        def finish(block):
            pltpu.make_async_copy(xrecv.at[block], xrecv.at[block], xrecv_sem.at[block]).wait()
            for unit in range(2):
                mine = key_rows_of(2 * block + unit, half_of(unit, core))
                to = aligned(block * rows + unit * half_rows, half_rows, half_rows)
                part = pl.ds(unit * half_rows, half_rows)
                stage[2, to] = ((dk[mine] + xrecv[block, 0, part].astype(F32)) * score_scale).astype(BF16)
                stage[3, to] = (dv[mine] + xrecv[block, 1, part].astype(F32)).astype(BF16)
            column = aligned((me_t * heads + head) * HSIZE, HSIZE, HSIZE)
            for unit in range(2):
                section = 2 * block + unit

                @pl.loop(0, half_rows // chunk)
                def _(index):
                    tensor = half_of(unit, core) * half_tensors + index
                    source = stage.at[:, aligned(block * rows + unit * half_rows + index * chunk, chunk, chunk)]
                    place = out_ref.at[:, :, column]
                    itself = jnp.logical_and(section == me_s, tensor == me_t)

                    @pl.when(jnp.logical_not(itself))
                    def _():
                        pltpu.make_async_remote_copy(
                            src_ref=source, dst_ref=place, send_sem=osend_sem, recv_sem=orecv_sem,
                            device_id={"section": section, "tensor": tensor}, device_id_type=MESH,
                        ).start()

                    @pl.when(itself)
                    def _():
                        pltpu.make_async_copy(source, place, orecv_sem).start()

        @pl.loop(0, blocks)
        def _(step):
            block = blocks - 1 - step
            own = own_span(block)
            piece = lane_q // CSLOT
            length = jnp.zeros((1, rows), jnp.int32)
            for unit in range(2):
                first = ((2 * block + unit) * rows + half_of(unit, core) * half_rows) // CSLOT
                for inner in range(half_rows // CSLOT):
                    length = jnp.where(
                        piece == unit * (half_rows // CSLOT) + inner, group_len_of(first + inner), length
                    )
            valid = lax.rem(lane_q, CSLOT) < length
            inverse = 1.0 / totals[block]
            keep = jnp.where(valid, inverse, 0.0)
            grad_t = gbuf[own].T.astype(F32) * keep
            out_t = outt[block]
            delta = jnp.sum(grad_t * out_t, axis=0, keepdims=True) * inverse
            stage[0, own] = (out_t * keep).T.astype(BF16)
            grad_low_t = grad_t.astype(BF16)
            grad_low = grad_t.T.astype(BF16)
            query_now = qbuf[own]
            dqt[...] = jnp.zeros((HSIZE, rows), F32)

            def grad_step(index, _):
                span = key_span(index)
                low = pbuf[p_span(block, index)]
                grad_scores = dot(vbuf[span], grad_low_t, (1, 0))
                score_grad = (low.astype(F32) * (grad_scores - delta)).astype(BF16)
                dv[span] += dot(low, grad_low, (1, 0))
                dk[span] += dot(score_grad, query_now, (1, 0))
                dqt[...] += dot(kt[:, span], score_grad, (1, 0))
                return 0

            lax.fori_loop(0, block + 1, grad_step, 0)
            stage[1, own] = (dqt[...] * score_scale).T.astype(BF16)
            for unit in range(2):
                theirs = key_rows_of(2 * block + unit, half_of(unit, 1 - core))
                part = pl.ds(unit * half_rows, half_rows)
                xsend[block, 0, part] = dk[theirs].astype(BF16)
                xsend[block, 1, part] = dv[theirs].astype(BF16)
            pltpu.make_async_remote_copy(
                src_ref=xsend.at[block], dst_ref=xrecv.at[block],
                send_sem=xsend_sem, recv_sem=xrecv_sem.at[block],
                device_id={"section": sibling}, device_id_type=MESH,
            ).start()

            @pl.when(step > 0)
            def _():
                finish(block + 1)

        finish(0)

        for kind in (0, 2):
            part = landing[kind].at[pl.ds(0, sections * half_rows)]
            pltpu.make_async_copy(part, part, fsend_sem.at[kind // 2]).wait()
        pltpu.make_async_copy(xsend, xsend, xsend_sem).wait()

        @pl.when(to_itself)
        def _():
            part = stage.at[:, pl.ds(0, sections * half_rows - chunk)]
            pltpu.make_async_copy(part, part, osend_sem).wait()

        @pl.when(jnp.logical_not(to_itself))
        def _():
            pltpu.make_async_copy(stage, stage, osend_sem).wait()

        for kind in range(4):
            part = vbuf.at[pl.ds(0, (2 * heads - 1) * half_rows)]
            pltpu.make_async_copy(part, part, send_sem.at[kind]).wait()

    @pl.when(jnp.logical_not(active))
    def _():
        for kind in range(4):
            part = vbuf.at[pl.ds(0, 2 * heads * half_rows)]
            pltpu.make_async_copy(part, part, send_sem.at[kind]).wait()

    pltpu.make_async_copy(out_ref, out_ref, orecv_sem).wait()


def per_device(query_in, key_in, value_in, out_grad, group_len):
    rows, columns = query_in.shape
    sections, tensors = lax.axis_size("section"), lax.axis_size("tensor")
    heads = columns // HSIZE
    chunk = rows // tensors
    seq_len = rows * sections
    own = seq_len // 2
    blocks = sections // 2
    tiles = blocks * (blocks + 1) // 2
    vmem = pltpu.VMEM
    dma = pltpu.SemaphoreType.DMA
    anywhere = pl.BlockSpec(memory_space=pl.ANY)
    out = pl.pallas_call(
        functools.partial(attention_kernel, sections, tensors, heads),
        out_shape=jax.ShapeDtypeStruct((4, chunk, columns * tensors), BF16),
        in_specs=[pl.BlockSpec(memory_space=pltpu.SMEM)] + [anywhere] * 4,
        out_specs=anywhere,
        scratch_shapes=[
            vmem((seq_len, HSIZE), BF16),
            vmem((seq_len, HSIZE), BF16),
            vmem((own, HSIZE), BF16),
            vmem((own, HSIZE), BF16),
            vmem((HSIZE, seq_len), BF16),
            vmem((HSIZE, seq_len), BF16),
            vmem((seq_len, HSIZE), BF16),
            vmem((rows, HSIZE), BF16),
            vmem((seq_len, rows), F32),
            vmem((tiles * 2 * rows, rows), BF16),
            vmem((blocks, HSIZE, rows), F32),
            vmem((blocks, 1, rows), F32),
            vmem((HSIZE, rows), F32),
            vmem((seq_len, HSIZE), F32),
            vmem((seq_len, HSIZE), F32),
            vmem((4, own, HSIZE), BF16),
            vmem((blocks, 2, rows, HSIZE), BF16),
            vmem((blocks, 2, rows, HSIZE), BF16),
            dma((4, sections)),
            dma((2, sections)),
            dma((4,)),
            dma((2,)),
            dma,
            dma((blocks,)),
            dma,
            dma,
        ],
        compiler_params=pltpu.CompilerParams(
            collective_id=0, has_side_effects=True, vmem_limit_bytes=56 * 1024 * 1024
        ),
        cost_estimate=pl.CostEstimate(
            flops=12 * HSIZE * seq_len * seq_len // 4,
            bytes_accessed=16 * rows * columns,
            transcendentals=seq_len * seq_len // 4,
        ),
    )(group_len, query_in, key_in, value_in, out_grad)
    return tuple(out[index] for index in range(4))


def solution(mesh):
    whole = P(("section", "tensor"), None)
    return jax.shard_map(
        per_device,
        mesh=mesh,
        in_specs=(P("section", "tensor"),) * 4 + (P(),),
        out_specs=(whole,) * 4,
        check_vma=False,
    )
```

time: 521 us -> 103 us (0.20); the launches traced: 515 us -> 103 us
  local copies, waits for them, and re-layouts: 156 us -> 2.51 us
  matrix products: 119 us -> 0 us
  Pallas kernels: 0 us -> 99.5 us
  other arithmetic: 80.2 us -> 0 us
  waiting for transfers between devices: 65.7 us -> 0 us
  blocking collectives: 37.9 us -> 0 us
  starting transfers between devices: 24.9 us -> 0 us
  loops' own time: 17.5 us -> 0 us
  between operations: 14 us -> 0.64 us
    dot_general x56 -> x0, matrix products: 119 us -> none  [the longest x8 34.5 us: grad_block_step(): jnp.einsum('qhk,khd->qhd', score_grad, key_block_h, preferred_element_typ...]
    dynamic_slice x72 -> x0, local copies, waits for them, and re-layouts: 110 us -> none  [the longest x16 38.4 us: key_block(): lax.dynamic_slice_in_dim(value_part, offset, block_rows)]
    pallas_call x0 -> x1, Pallas kernels: none -> 99.5 us  [per_device(): pl.pallas_call(functools.partial(attention_kernel, sections, tensors, hea...]
    all_gather x4 -> x0, waiting for transfers between devices: 55.8 us -> none  [the longest x1 54.9 us: per_device(): lax.all_gather(value_in, 'section', axis=0, tiled=True)]
    all_gather x2 -> x0, blocking collectives: 37.9 us -> none  [the longest x1 19.3 us: per_device(): lax.all_gather(log_total, 'section', axis=0, tiled=True)]
    lt x1 -> x0, other arithmetic: 36.4 us -> none  [per_device(): is_valid = positions % CSLOT < slot_lens]
    all_to_all x4 -> x0, starting transfers between devices: 24.7 us -> none  [the longest x1 6.97 us: per_device(): lax.all_to_all(query_flat, 'tensor', split_axis=0, concat_axis=1, tiled=T...]
    while x184 -> x0, local copies, waits for them, and re-layouts: 21.4 us -> none
  transfers between devices with their start and end apart: 8 -> 0, of which waited for: 4 -> 0; matrix products, arithmetic and copies ran while one was open for 64% -> 0% of each run, Pallas kernels for 0% -> 0%
where the time goes in v1:
time: 103 us
  Pallas kernels  99.5 us (97%)
  local copies, waits for them, and re-layouts  2.51 us (2%)
    pallas_call x1, Pallas kernels, per_device(): pl.pallas_call(functools.partial(attention_kernel, sections, tensors, hea...  99.5 us
    squeeze x1, local copies, waits for them, and re-layouts, per_device(): return tuple((out[index] for index in range(4)))  2.51 us

profile of v1, /device:TPU:1, one launch (start us, length us, event | category | flops | bytes accessed | tf_op | source)
XLA Modules:
  0.0 102.6 jit_solution(11199389870317427073)
XLA Ops:
  0.6 99.5 %shard_map.84 = bf16[4,32,6144]{2,1,0:T(8,128)(2,1)} custom-call(s32[64]{0:T(128)} %len_ref.1, bf16[256,768]{1,0:T(8,128)(2,1)} %q_ref.1, bf16[256,768]{1,0:T(8,128)(2,1)} %k_ref.1, bf16[256,768]{1,0:T(8,128)(2,1)} %v_ref.1, bf16[256,768]{1,0:T(8,128)(2,1)} %g_ref.1), custom_call_target="tpu_custom_call" | custom-call | flops 6442450944 | bytes 3145728 | tf_op jit(solution)/shard_map/pallas_call | solution.py:377
  100.1 2.5 %slice_bitcast_fusion = (bf16[32,6144]{1,0:T(8,128)(2,1)}, bf16[32,6144]{1,0:T(8,128)(2,1)}, bf16[32,6144]{1,0:T(8,128)(2,1)}, bf16[32,6144]{1,0:T(8,128)(2,1)}) fusion(bf16[4,32,6144]{2,1,0:T(8,128)(2,1)} %shard_map.84), kind=kLoop, calls=%fused_computation | loop fusion | bytes 3145728 | tf_op jit(solution)/shard_map/squeeze | solution.py:419

commit v2 on v1

--- a/solution.py
+++ b/solution.py
@@ -19,8 +19,8 @@
 def chip_of(head, tensor, chips):
     if chips != 8:
         return lax.rem(head + tensor, chips)
-    level = head // 3
-    x = lax.rem(lax.rem(head, 3) + 2 * level + tensor // 2, 4)
+    level = head // 4
+    x = lax.rem((1 + level) * lax.rem(head, 4) + tensor // 2, 4)
     return 2 * x + level
 
 
@@ -29,8 +29,11 @@
         head = lax.rem(chip - lax.rem(tensor, chips) + chips, chips)
         return (head, head < heads)
     level = lax.rem(chip, 2)
-    place = lax.rem(chip // 2 + 8 - 2 * level - tensor // 2, 4)
-    return (3 * level + place, place < 3)
+    place = lax.rem(chip // 2 + 4 - tensor // 2, 4)
+    return (
+        jnp.where(level == 0, place, 4 + place // 2),
+        jnp.logical_or(level == 0, lax.rem(place, 2) == 0),
+    )
 
 
 def dot(a, b, dims):
@@ -40,9 +43,9 @@
 def attention_kernel(
     sections, tensors, heads,
     len_ref, q_ref, k_ref, v_ref, g_ref, out_ref,
-    kbuf, vbuf, qbuf, gbuf, kt, vt, bias, ones, sbuf, pbuf, outt, totals, dqt, dk, dv,
+    kbuf, vbuf, qbuf, gbuf, kt, vt, bias, ones, sbuf, pbuf, outt, tops, totals, dqt, dk, dv,
     stage, xsend, xrecv,
-    recv_sem, fwd_sem, send_sem, fsend_sem, xsend_sem, xrecv_sem, osend_sem, orecv_sem,
+    recv_sem, fwd_sem, send_sem, fsend_sem, xsend_sem, xrecv_sem, osend_sem, orecv_sem, entered,
 ):
     rows = q_ref.shape[0]
     half_rows = rows // 2
@@ -78,35 +81,16 @@
         return landing[kind].at[key_rows_of(section, half) if kind in (0, 2) else own_rows_of(section)]
 
     barrier = pltpu.get_barrier_semaphore()
-
-    @pl.when(active)
-    def _():
-        @pl.loop(1, sections)
-        def _(step):
-            pl.semaphore_signal(
-                barrier, inc=1, device_id={"section": lax.rem(me_s + step, sections)}, device_id_type=MESH
-            )
-
-    out_core = lax.rem(core + me_t // half_tensors, 2)
-
-    @pl.loop(0, tensors)
-    def _(tensor):
-        @pl.loop(0, heads)
-        def _(index):
-            target = 2 * chip_of(index, tensor, chips) + out_core
-
-            @pl.when(jnp.logical_or(target != me_s, tensor != me_t))
-            def _():
-                pl.semaphore_signal(
-                    barrier, inc=1, device_id={"section": target, "tensor": tensor}, device_id_type=MESH
-                )
-
-    to_itself = me_t < half_tensors
-    is_active = active.astype(jnp.int32)
-    pl.semaphore_wait(
-        barrier,
-        2 * heads - is_active + is_active * (sections * half_tensors - to_itself.astype(jnp.int32)),
-    )
+    steps = [1 << bit for bit in range(tensors.bit_length() - 1)]
+    for step in range(1, sections):
+        pl.semaphore_signal(
+            barrier, inc=1, device_id={"section": jnp.bitwise_xor(me_s, step)}, device_id_type=MESH
+        )
+    for step in steps:
+        pl.semaphore_signal(
+            barrier, inc=1, device_id={"tensor": jnp.bitwise_xor(me_t, step)}, device_id_type=MESH
+        )
+    pl.semaphore_wait(barrier, sections - 1 + len(steps))
 
     for kind in range(4):
         @pl.loop(0, heads)
@@ -168,6 +152,14 @@
     def group_len_of(group):
         return len_ref[group]
 
+    for bit, step in enumerate(steps):
+        pl.semaphore_signal(
+            entered.at[bit], inc=1, device_id={"tensor": jnp.bitwise_xor(me_t, step)}, device_id_type=MESH
+        )
+        pl.semaphore_wait(entered.at[bit], 1)
+
+    to_itself = me_t < half_tensors
+
     @pl.when(active)
     def _():
         lane = lax.broadcasted_iota(jnp.int32, (CSLOT, HSIZE), 1)
@@ -194,15 +186,7 @@
         def _(section):
             wait_arrival(1, section)
 
-        forward(2)
         wait_forwarded(0)
-        wait_forwarded(2)
-
-        @pl.loop(0, blocks)
-        def _(block):
-            span = aligned(block * key_rows, key_rows, key_rows)
-            kt[:, span] = kbuf[span].T
-            vt[:, span] = vbuf[span].T
 
         def p_span(block, index):
             return aligned((block * (block + 1) // 2 + index) * key_rows, key_rows, key_rows)
@@ -218,8 +202,46 @@
             lane_q < half_rows, core * half_rows + lane_q, rows + (1 - core) * half_rows + lane_q - half_rows
         )
 
+        def send_out(block, first, last, group):
+            column = aligned((me_t * heads + head) * HSIZE, HSIZE, HSIZE)
+            for unit in range(2):
+                section = 2 * block + unit
+
+                @pl.loop(0, half_rows // chunk)
+                def _(index):
+                    tensor = half_of(unit, core) * half_tensors + index
+                    start = block * rows + unit * half_rows + index * chunk
+                    source = stage.at[pl.ds(first, last - first), aligned(start, chunk, chunk)]
+                    place = out_ref.at[pl.ds(first, last - first), :, column]
+                    itself = jnp.logical_and(section == me_s, tensor == me_t)
+
+                    @pl.when(jnp.logical_not(itself))
+                    def _():
+                        pltpu.make_async_remote_copy(
+                            src_ref=source, dst_ref=place,
+                            send_sem=osend_sem.at[group], recv_sem=orecv_sem.at[group],
+                            device_id={"section": section, "tensor": tensor}, device_id_type=MESH,
+                        ).start()
+
+                    @pl.when(itself)
+                    def _():
+                        pltpu.make_async_copy(source, place, orecv_sem.at[group]).start()
+
+        def valid_rows(block):
+            piece = lane_q // CSLOT
+            length = jnp.zeros((1, rows), jnp.int32)
+            for unit in range(2):
+                first = ((2 * block + unit) * rows + half_of(unit, core) * half_rows) // CSLOT
+                for inner in range(half_rows // CSLOT):
+                    length = jnp.where(
+                        piece == unit * (half_rows // CSLOT) + inner, group_len_of(first + inner), length
+                    )
+            return lax.rem(lane_q, CSLOT) < length
+
         @pl.loop(0, blocks)
         def _(block):
+            span = key_span(block)
+            kt[:, span] = kbuf[span].T
             query_wide = jnp.concatenate([qbuf[own_span(block)], ones[...]], axis=1)
 
             def score_step(index, top, diagonal=False):
@@ -229,24 +251,35 @@
                 if diagonal:
                     place = lax.broadcasted_iota(jnp.int32, (key_rows, rows), 0)
                     scores = jnp.where(place <= query_place, scores, NEG_FILL)
-                sbuf[span] = scores
+                sbuf[p_span(block, index)] = scores
                 return jnp.maximum(top, jnp.max(scores.reshape(key_rows // 8, 8, rows), axis=0))
 
             top = lax.fori_loop(0, block, score_step, jnp.full((8, rows), NEG_FILL, F32))
-            top = score_step(block, top, diagonal=True)
-            shift = jnp.max(top, axis=0, keepdims=True) * exp_scale
+            tops[block] = score_step(block, top, diagonal=True)
+
+        forward(2)
+        wait_forwarded(2)
+
+        @pl.loop(0, blocks)
+        def _(block):
+            span = key_span(block)
+            vt[:, span] = vbuf[span].T
+            shift = jnp.max(tops[block], axis=0, keepdims=True) * exp_scale
             outt[block] = jnp.zeros((HSIZE, rows), F32)
 
             def weight_step(index, total):
-                span = key_span(index)
-                weights = jnp.exp2(sbuf[span] * exp_scale - shift)
+                weights = jnp.exp2(sbuf[p_span(block, index)] * exp_scale - shift)
                 low = weights.astype(BF16)
                 pbuf[p_span(block, index)] = low
-                outt[block] += dot(vt[:, span], low, (1, 0))
+                outt[block] += dot(vt[:, key_span(index)], low, (1, 0))
                 return total + jnp.sum(weights.reshape(key_rows // 8, 8, rows), axis=0)
 
             total = lax.fori_loop(0, block + 1, weight_step, jnp.zeros((8, rows), F32))
-            totals[block] = jnp.sum(total, axis=0, keepdims=True)
+            total = jnp.sum(total, axis=0, keepdims=True)
+            totals[block] = total
+            keep = jnp.where(valid_rows(block), 1.0 / total, 0.0)
+            stage[0, own_span(block)] = (outt[block] * keep).T.astype(BF16)
+            send_out(block, 0, 1, 0)
 
         @pl.loop(0, sections)
         def _(section):
@@ -260,47 +293,17 @@
                 part = pl.ds(unit * half_rows, half_rows)
                 stage[2, to] = ((dk[mine] + xrecv[block, 0, part].astype(F32)) * score_scale).astype(BF16)
                 stage[3, to] = (dv[mine] + xrecv[block, 1, part].astype(F32)).astype(BF16)
-            column = aligned((me_t * heads + head) * HSIZE, HSIZE, HSIZE)
-            for unit in range(2):
-                section = 2 * block + unit
-
-                @pl.loop(0, half_rows // chunk)
-                def _(index):
-                    tensor = half_of(unit, core) * half_tensors + index
-                    source = stage.at[:, aligned(block * rows + unit * half_rows + index * chunk, chunk, chunk)]
-                    place = out_ref.at[:, :, column]
-                    itself = jnp.logical_and(section == me_s, tensor == me_t)
-
-                    @pl.when(jnp.logical_not(itself))
-                    def _():
-                        pltpu.make_async_remote_copy(
-                            src_ref=source, dst_ref=place, send_sem=osend_sem, recv_sem=orecv_sem,
-                            device_id={"section": section, "tensor": tensor}, device_id_type=MESH,
-                        ).start()
-
-                    @pl.when(itself)
-                    def _():
-                        pltpu.make_async_copy(source, place, orecv_sem).start()
+            send_out(block, 1, 4, 1)
 
         @pl.loop(0, blocks)
         def _(step):
             block = blocks - 1 - step
             own = own_span(block)
-            piece = lane_q // CSLOT
-            length = jnp.zeros((1, rows), jnp.int32)
-            for unit in range(2):
-                first = ((2 * block + unit) * rows + half_of(unit, core) * half_rows) // CSLOT
-                for inner in range(half_rows // CSLOT):
-                    length = jnp.where(
-                        piece == unit * (half_rows // CSLOT) + inner, group_len_of(first + inner), length
-                    )
-            valid = lax.rem(lane_q, CSLOT) < length
             inverse = 1.0 / totals[block]
-            keep = jnp.where(valid, inverse, 0.0)
+            keep = jnp.where(valid_rows(block), inverse, 0.0)
             grad_t = gbuf[own].T.astype(F32) * keep
             out_t = outt[block]
             delta = jnp.sum(grad_t * out_t, axis=0, keepdims=True) * inverse
-            stage[0, own] = (out_t * keep).T.astype(BF16)
             grad_low_t = grad_t.astype(BF16)
             grad_low = grad_t.T.astype(BF16)
             query_now = qbuf[own]
@@ -340,14 +343,17 @@
             pltpu.make_async_copy(part, part, fsend_sem.at[kind // 2]).wait()
         pltpu.make_async_copy(xsend, xsend, xsend_sem).wait()
 
-        @pl.when(to_itself)
-        def _():
-            part = stage.at[:, pl.ds(0, sections * half_rows - chunk)]
-            pltpu.make_async_copy(part, part, osend_sem).wait()
-
-        @pl.when(jnp.logical_not(to_itself))
-        def _():
-            pltpu.make_async_copy(stage, stage, osend_sem).wait()
+        own_rows = sections * half_rows
+        for group, (first, last) in enumerate(((0, 1), (1, 4))):
+            @pl.when(to_itself)
+            def _():
+                part = stage.at[pl.ds(first, last - first), pl.ds(0, own_rows - chunk)]
+                pltpu.make_async_copy(part, part, osend_sem.at[group]).wait()
+
+            @pl.when(jnp.logical_not(to_itself))
+            def _():
+                part = stage.at[pl.ds(first, last - first)]
+                pltpu.make_async_copy(part, part, osend_sem.at[group]).wait()
 
         for kind in range(4):
             part = vbuf.at[pl.ds(0, (2 * heads - 1) * half_rows)]
@@ -359,7 +365,9 @@
             part = vbuf.at[pl.ds(0, 2 * heads * half_rows)]
             pltpu.make_async_copy(part, part, send_sem.at[kind]).wait()
 
-    pltpu.make_async_copy(out_ref, out_ref, orecv_sem).wait()
+    for group, (first, last) in enumerate(((0, 1), (1, 4))):
+        part = out_ref.at[pl.ds(first, last - first)]
+        pltpu.make_async_copy(part, part, orecv_sem.at[group]).wait()
 
 
 def per_device(query_in, key_in, value_in, out_grad, group_len):
@@ -388,9 +396,10 @@
             vmem((HSIZE, seq_len), BF16),
             vmem((seq_len, HSIZE), BF16),
             vmem((rows, HSIZE), BF16),
-            vmem((seq_len, rows), F32),
+            vmem((tiles * 2 * rows, rows), F32),
             vmem((tiles * 2 * rows, rows), BF16),
             vmem((blocks, HSIZE, rows), F32),
+            vmem((blocks, 8, rows), F32),
             vmem((blocks, 1, rows), F32),
             vmem((HSIZE, rows), F32),
             vmem((seq_len, HSIZE), F32),
@@ -404,8 +413,9 @@
             dma((2,)),
             dma,
             dma((blocks,)),
-            dma,
-            dma,
+            dma((2,)),
+            dma((2,)),
+            pltpu.SemaphoreType.REGULAR((tensors.bit_length() - 1,)),
         ],
         compiler_params=pltpu.CompilerParams(
             collective_id=0, has_side_effects=True, vmem_limit_bytes=56 * 1024 * 1024

time: 103 us -> 96.1 us (0.933)
  Pallas kernels: 99.5 us -> 92.8 us
    pallas_call x1, Pallas kernels: 99.5 us -> 92.8 us  [per_device(): pl.pallas_call(functools.partial(attention_kernel, sections, tensors, hea...]
where the time goes in v2:
time: 96.1 us; the launch traced here: 96 us
  Pallas kernels  92.8 us (97%)
  local copies, waits for them, and re-layouts  2.51 us (3%)
    pallas_call x1, Pallas kernels, per_device(): pl.pallas_call(functools.partial(attention_kernel, sections, tensors, hea...  92.8 us
    squeeze x1, local copies, waits for them, and re-layouts, per_device(): return tuple((out[index] for index in range(4)))  2.51 us

profile of v2, /device:TPU:1, one launch (start us, length us, event | category | flops | bytes accessed | tf_op | source)
XLA Modules:
  0.0 96.0 jit_solution(2668406081423075686)
XLA Ops:
  0.6 92.8 %shard_map.84 = bf16[4,32,6144]{2,1,0:T(8,128)(2,1)} custom-call(s32[64]{0:T(128)} %len_ref.1, bf16[256,768]{1,0:T(8,128)(2,1)} %q_ref.1, bf16[256,768]{1,0:T(8,128)(2,1)} %k_ref.1, bf16[256,768]{1,0:T(8,128)(2,1)} %v_ref.1, bf16[256,768]{1,0:T(8,128)(2,1)} %g_ref.1), custom_call_target="tpu_custom_call" | custom-call | flops 6442450944 | bytes 3145728 | tf_op jit(solution)/shard_map/pallas_call | solution.py:385
  93.5 2.5 %slice_bitcast_fusion = (bf16[32,6144]{1,0:T(8,128)(2,1)}, bf16[32,6144]{1,0:T(8,128)(2,1)}, bf16[32,6144]{1,0:T(8,128)(2,1)}, bf16[32,6144]{1,0:T(8,128)(2,1)}) fusion(bf16[4,32,6144]{2,1,0:T(8,128)(2,1)} %shard_map.84), kind=kLoop, calls=%fused_computation | loop fusion | bytes 3145728 | tf_op jit(solution)/shard_map/squeeze | solution.py:429

commit v3 on v2

--- a/solution.py
+++ b/solution.py
@@ -43,7 +43,7 @@
 def attention_kernel(
     sections, tensors, heads,
     len_ref, q_ref, k_ref, v_ref, g_ref, out_ref,
-    kbuf, vbuf, qbuf, gbuf, kt, vt, bias, ones, sbuf, pbuf, outt, tops, totals, dqt, dk, dv,
+    kbuf, vbuf, qbuf, gbuf, kt, vt, bias, ones, sbuf, pbuf, outt, tops, totals, dk, dv,
     stage, xsend, xrecv,
     recv_sem, fwd_sem, send_sem, fsend_sem, xsend_sem, xrecv_sem, osend_sem, orecv_sem, entered,
 ):
@@ -92,9 +92,9 @@
         )
     pl.semaphore_wait(barrier, sections - 1 + len(steps))
 
-    for kind in range(4):
+    def send_kind(kind):
         @pl.loop(0, heads)
-        def _(step, kind=kind):
+        def _(step):
             index = lax.rem(step + me_s // 2, heads)
             chip = chip_of(index, me_t, chips)
             for half_step in range(2):
@@ -124,6 +124,17 @@
                 else:
                     send()
 
+    def wait_sent(kind):
+        @pl.when(active)
+        def _():
+            part = vbuf.at[pl.ds(0, (2 * heads - 1) * half_rows)]
+            pltpu.make_async_copy(part, part, send_sem.at[kind]).wait()
+
+        @pl.when(jnp.logical_not(active))
+        def _():
+            part = vbuf.at[pl.ds(0, 2 * heads * half_rows)]
+            pltpu.make_async_copy(part, part, send_sem.at[kind]).wait()
+
     def wait_arrival(kind, section):
         place = slot(kind, section, half_of(section, core))
         pltpu.make_async_copy(place, place, recv_sem.at[kind, section]).wait()
@@ -149,6 +160,11 @@
             place = slot(kind, section, half_of(section, 1 - core))
             pltpu.make_async_copy(place, place, fwd_sem.at[which, section]).wait()
 
+    send_kind(0)
+    send_kind(1)
+    wait_sent(0)
+    send_kind(2)
+
     def group_len_of(group):
         return len_ref[group]
 
@@ -174,28 +190,27 @@
             lax.broadcasted_iota(jnp.int32, ones.shape, 1) == 0, 1.0, 0.0
         ).astype(BF16)
 
-        @pl.loop(0, blocks)
-        def _(block):
-            span = aligned(block * key_rows, key_rows, key_rows)
-            dk[span] = jnp.zeros((key_rows, HSIZE), F32)
-            dv[span] = jnp.zeros((key_rows, HSIZE), F32)
-
         forward(0)
 
+    wait_sent(1)
+    send_kind(3)
+
+    @pl.when(active)
+    def _():
         @pl.loop(0, sections)
         def _(section):
             wait_arrival(1, section)
 
         wait_forwarded(0)
 
-        def p_span(block, index):
-            return aligned((block * (block + 1) // 2 + index) * key_rows, key_rows, key_rows)
-
-        def key_span(index):
-            return aligned(index * key_rows, key_rows, key_rows)
+        def p_span(block, index, count=1):
+            return pl.ds((block * (block + 1) // 2 + index) * key_rows, count * key_rows)
+
+        def key_span(index, count=1):
+            return pl.ds(index * key_rows, count * key_rows)
 
         def own_span(block):
-            return aligned(block * rows, rows, rows)
+            return pl.ds(block * rows, rows)
 
         lane_q = lax.broadcasted_iota(jnp.int32, (1, rows), 1)
         query_place = jnp.where(
@@ -238,47 +253,39 @@
                     )
             return lax.rem(lane_q, CSLOT) < length
 
-        @pl.loop(0, blocks)
-        def _(block):
+        for block in range(blocks):
             span = key_span(block)
             kt[:, span] = kbuf[span].T
             query_wide = jnp.concatenate([qbuf[own_span(block)], ones[...]], axis=1)
 
-            def score_step(index, top, diagonal=False):
+            top = jnp.full((8, rows), NEG_FILL, F32)
+            for index in range(block + 1):
                 span = key_span(index)
                 key_wide = jnp.concatenate([kbuf[span], bias[span]], axis=1)
                 scores = dot(key_wide, query_wide, (1, 1))
-                if diagonal:
+                if index == block:
                     place = lax.broadcasted_iota(jnp.int32, (key_rows, rows), 0)
                     scores = jnp.where(place <= query_place, scores, NEG_FILL)
                 sbuf[p_span(block, index)] = scores
-                return jnp.maximum(top, jnp.max(scores.reshape(key_rows // 8, 8, rows), axis=0))
-
-            top = lax.fori_loop(0, block, score_step, jnp.full((8, rows), NEG_FILL, F32))
-            tops[block] = score_step(block, top, diagonal=True)
+                top = jnp.maximum(top, jnp.max(scores.reshape(key_rows // 8, 8, rows), axis=0))
+            tops[block] = top
 
         forward(2)
         wait_forwarded(2)
 
-        @pl.loop(0, blocks)
-        def _(block):
+        for block in range(blocks):
             span = key_span(block)
             vt[:, span] = vbuf[span].T
             shift = jnp.max(tops[block], axis=0, keepdims=True) * exp_scale
-            outt[block] = jnp.zeros((HSIZE, rows), F32)
-
-            def weight_step(index, total):
-                weights = jnp.exp2(sbuf[p_span(block, index)] * exp_scale - shift)
-                low = weights.astype(BF16)
-                pbuf[p_span(block, index)] = low
-                outt[block] += dot(vt[:, key_span(index)], low, (1, 0))
-                return total + jnp.sum(weights.reshape(key_rows // 8, 8, rows), axis=0)
-
-            total = lax.fori_loop(0, block + 1, weight_step, jnp.zeros((8, rows), F32))
-            total = jnp.sum(total, axis=0, keepdims=True)
+            weights = jnp.exp2(sbuf[p_span(block, 0, block + 1)] * exp_scale - shift)
+            low = weights.astype(BF16)
+            pbuf[p_span(block, 0, block + 1)] = low
+            total = jnp.sum(weights, axis=0, keepdims=True)
             totals[block] = total
+            out_t = dot(vt[:, key_span(0, block + 1)], low, (1, 0))
+            outt[block] = out_t
             keep = jnp.where(valid_rows(block), 1.0 / total, 0.0)
-            stage[0, own_span(block)] = (outt[block] * keep).T.astype(BF16)
+            stage[0, own_span(block)] = (out_t * keep).T.astype(BF16)
             send_out(block, 0, 1, 0)
 
         @pl.loop(0, sections)
@@ -295,9 +302,7 @@
                 stage[3, to] = (dv[mine] + xrecv[block, 1, part].astype(F32)).astype(BF16)
             send_out(block, 1, 4, 1)
 
-        @pl.loop(0, blocks)
-        def _(step):
-            block = blocks - 1 - step
+        for block in reversed(range(blocks)):
             own = own_span(block)
             inverse = 1.0 / totals[block]
             keep = jnp.where(valid_rows(block), inverse, 0.0)
@@ -307,20 +312,19 @@
             grad_low_t = grad_t.astype(BF16)
             grad_low = grad_t.T.astype(BF16)
             query_now = qbuf[own]
-            dqt[...] = jnp.zeros((HSIZE, rows), F32)
-
-            def grad_step(index, _):
-                span = key_span(index)
-                low = pbuf[p_span(block, index)]
+            dq_t = jnp.zeros((HSIZE, rows), F32)
+            for index in range(0, block + 1, 2):
+                count = min(2, block + 1 - index)
+                span = key_span(index, count)
+                low = pbuf[p_span(block, index, count)]
                 grad_scores = dot(vbuf[span], grad_low_t, (1, 0))
                 score_grad = (low.astype(F32) * (grad_scores - delta)).astype(BF16)
-                dv[span] += dot(low, grad_low, (1, 0))
-                dk[span] += dot(score_grad, query_now, (1, 0))
-                dqt[...] += dot(kt[:, span], score_grad, (1, 0))
-                return 0
-
-            lax.fori_loop(0, block + 1, grad_step, 0)
-            stage[1, own] = (dqt[...] * score_scale).T.astype(BF16)
+                dv_part = dot(low, grad_low, (1, 0))
+                dk_part = dot(score_grad, query_now, (1, 0))
+                dv[span] = dv_part if block == blocks - 1 else dv[span] + dv_part
+                dk[span] = dk_part if block == blocks - 1 else dk[span] + dk_part
+                dq_t += dot(kt[:, span], score_grad, (1, 0))
+            stage[1, own] = (dq_t * score_scale).T.astype(BF16)
             for unit in range(2):
                 theirs = key_rows_of(2 * block + unit, half_of(unit, 1 - core))
                 part = pl.ds(unit * half_rows, half_rows)
@@ -332,8 +336,7 @@
                 device_id={"section": sibling}, device_id_type=MESH,
             ).start()
 
-            @pl.when(step > 0)
-            def _():
+            if block < blocks - 1:
                 finish(block + 1)
 
         finish(0)
@@ -355,16 +358,8 @@
                 part = stage.at[pl.ds(first, last - first)]
                 pltpu.make_async_copy(part, part, osend_sem.at[group]).wait()
 
-        for kind in range(4):
-            part = vbuf.at[pl.ds(0, (2 * heads - 1) * half_rows)]
-            pltpu.make_async_copy(part, part, send_sem.at[kind]).wait()
-
-    @pl.when(jnp.logical_not(active))
-    def _():
-        for kind in range(4):
-            part = vbuf.at[pl.ds(0, 2 * heads * half_rows)]
-            pltpu.make_async_copy(part, part, send_sem.at[kind]).wait()
-
+    wait_sent(2)
+    wait_sent(3)
     for group, (first, last) in enumerate(((0, 1), (1, 4))):
         part = out_ref.at[pl.ds(first, last - first)]
         pltpu.make_async_copy(part, part, orecv_sem.at[group]).wait()
@@ -401,7 +396,6 @@
             vmem((blocks, HSIZE, rows), F32),
             vmem((blocks, 8, rows), F32),
             vmem((blocks, 1, rows), F32),
-            vmem((HSIZE, rows), F32),
             vmem((seq_len, HSIZE), F32),
             vmem((seq_len, HSIZE), F32),
             vmem((4, own, HSIZE), BF16),

time: 96.1 us -> 76.3 us (0.79)
  Pallas kernels: 92.8 us -> 73 us
    pallas_call x1, Pallas kernels: 92.8 us -> 73 us  [per_device(): pl.pallas_call(functools.partial(attention_kernel, sections, tensors, hea...]
where the time goes in v3:
time: 76.3 us; the launch traced here: 76.2 us
  Pallas kernels  73 us (96%)
  local copies, waits for them, and re-layouts  2.51 us (3%)
    pallas_call x1, Pallas kernels, per_device(): pl.pallas_call(functools.partial(attention_kernel, sections, tensors, hea...  73 us
    squeeze x1, local copies, waits for them, and re-layouts, per_device(): return tuple((out[index] for index in range(4)))  2.51 us

profile of v3, /device:TPU:1, one launch (start us, length us, event | category | flops | bytes accessed | tf_op | source)
XLA Modules:
  0.0 76.2 jit_solution(15385169108032479161)
XLA Ops:
  0.6 73.0 %shard_map.84 = bf16[4,32,6144]{2,1,0:T(8,128)(2,1)} custom-call(s32[64]{0:T(128)} %len_ref.1, bf16[256,768]{1,0:T(8,128)(2,1)} %q_ref.1, bf16[256,768]{1,0:T(8,128)(2,1)} %k_ref.1, bf16[256,768]{1,0:T(8,128)(2,1)} %v_ref.1, bf16[256,768]{1,0:T(8,128)(2,1)} %g_ref.1), custom_call_target="tpu_custom_call" | custom-call | flops 6442450944 | bytes 3145728 | tf_op jit(solution)/shard_map/pallas_call | solution.py:380
  73.7 2.5 %slice_bitcast_fusion = (bf16[32,6144]{1,0:T(8,128)(2,1)}, bf16[32,6144]{1,0:T(8,128)(2,1)}, bf16[32,6144]{1,0:T(8,128)(2,1)}, bf16[32,6144]{1,0:T(8,128)(2,1)}) fusion(bf16[4,32,6144]{2,1,0:T(8,128)(2,1)} %shard_map.84), kind=kLoop, calls=%fused_computation | loop fusion | bytes 3145728 | tf_op jit(solution)/shard_map/squeeze | solution.py:423

commit v4 on v3

--- a/solution.py
+++ b/solution.py
@@ -19,21 +19,25 @@
 def chip_of(head, tensor, chips):
     if chips != 8:
         return lax.rem(head + tensor, chips)
-    level = head // 4
-    x = lax.rem((1 + level) * lax.rem(head, 4) + tensor // 2, 4)
-    return 2 * x + level
+    level = (head >= 3).astype(jnp.int32)
+    return 2 * (head - level + (tensor >> 1) & 3) + level
+
+
+def section_at(section, step, sections):
+    if sections != 16:
+        return lax.rem(section + step + 1, sections)
+    turn = step >> 2
+    shift = jnp.where(turn == 0, 2, jnp.where(turn == 1, 1, jnp.where(turn == 2, 3, 0)))
+    return 4 * ((section >> 2) + shift & 3) + (section + step & 3)
 
 
 def head_at(chip, tensor, chips, heads):
     if chips != 8:
         head = lax.rem(chip - lax.rem(tensor, chips) + chips, chips)
         return (head, head < heads)
-    level = lax.rem(chip, 2)
-    place = lax.rem(chip // 2 + 4 - tensor // 2, 4)
-    return (
-        jnp.where(level == 0, place, 4 + place // 2),
-        jnp.logical_or(level == 0, lax.rem(place, 2) == 0),
-    )
+    level = chip & 1
+    place = (chip >> 1) + 8 - 2 * level - (tensor >> 1) & 3
+    return (3 * level + place, place < 3)
 
 
 def dot(a, b, dims):
@@ -43,7 +47,7 @@
 def attention_kernel(
     sections, tensors, heads,
     len_ref, q_ref, k_ref, v_ref, g_ref, out_ref,
-    kbuf, vbuf, qbuf, gbuf, kt, vt, bias, ones, sbuf, pbuf, outt, tops, totals, dk, dv,
+    kbuf, vbuf, qbuf, gbuf, kt, vt, bias, ones, sbuf, pbuf, outt, tops, totals, valid, dk, dv,
     stage, xsend, xrecv,
     recv_sem, fwd_sem, send_sem, fsend_sem, xsend_sem, xrecv_sem, osend_sem, orecv_sem, entered,
 ):
@@ -59,7 +63,7 @@
 
     me_s = lax.axis_index("section")
     me_t = lax.axis_index("tensor")
-    core = lax.rem(me_s, 2)
+    core = me_s & 1
     sibling = me_s + 1 - 2 * core
     head, active = head_at(me_s // 2, me_t, chips, heads)
     inputs = (k_ref, q_ref, v_ref, g_ref)
@@ -69,7 +73,7 @@
         return pl.ds(pl.multiple_of(start, step), size)
 
     def half_of(section, of_core):
-        return lax.rem(of_core + section, 2)
+        return (of_core + section) & 1
 
     def key_rows_of(section, half):
         return aligned(section * rows + half * half_rows, half_rows, half_rows)
@@ -79,6 +83,62 @@
 
     def slot(kind, section, half):
         return landing[kind].at[key_rows_of(section, half) if kind in (0, 2) else own_rows_of(section)]
+
+    def group_len_of(group):
+        return len_ref[group]
+
+    def p_span(block, index, count=1):
+        return pl.ds((block * (block + 1) // 2 + index) * key_rows, count * key_rows)
+
+    def key_span(index, count=1):
+        return pl.ds(index * key_rows, count * key_rows)
+
+    def own_span(block):
+        return pl.ds(block * rows, rows)
+
+    lane_q = lax.broadcasted_iota(jnp.int32, (1, rows), 1)
+    query_place = jnp.where(
+        lane_q < half_rows, core * half_rows + lane_q, rows + (1 - core) * half_rows + lane_q - half_rows
+    )
+
+    def send_out(first, last, group, block=None):
+        column = aligned((me_t * heads + head) * HSIZE, HSIZE, HSIZE)
+
+        @pl.loop(0, sections if block is None else 2)
+        def _(step):
+            section = section_at(me_s, step, sections) if block is None else 2 * block + step
+
+            @pl.loop(0, half_rows // chunk)
+            def _(index):
+                tensor = half_of(section, core) * half_tensors + index
+                source = stage.at[
+                    pl.ds(first, last - first), aligned(section * half_rows + index * chunk, chunk, chunk)
+                ]
+                place = out_ref.at[pl.ds(first, last - first), :, column]
+                itself = jnp.logical_and(section == me_s, tensor == me_t)
+
+                @pl.when(jnp.logical_not(itself))
+                def _():
+                    pltpu.make_async_remote_copy(
+                        src_ref=source, dst_ref=place,
+                        send_sem=osend_sem.at[group], recv_sem=orecv_sem.at[group],
+                        device_id={"section": section, "tensor": tensor}, device_id_type=MESH,
+                    ).start()
+
+                @pl.when(itself)
+                def _():
+                    pltpu.make_async_copy(source, place, orecv_sem.at[group]).start()
+
+    def valid_rows(block):
+        piece = lane_q // CSLOT
+        length = jnp.zeros((1, rows), jnp.int32)
+        for unit in range(2):
+            first = (2 * block + unit) * (rows // CSLOT) + half_of(unit, core) * (half_rows // CSLOT)
+            for inner in range(half_rows // CSLOT):
+                length = jnp.where(
+                    piece == unit * (half_rows // CSLOT) + inner, group_len_of(first + inner), length
+                )
+        return jnp.where((lane_q & (CSLOT - 1)) < length, 1.0, 0.0).astype(F32)
 
     barrier = pltpu.get_barrier_semaphore()
     steps = [1 << bit for bit in range(tensors.bit_length() - 1)]
@@ -90,12 +150,43 @@
         pl.semaphore_signal(
             barrier, inc=1, device_id={"tensor": jnp.bitwise_xor(me_t, step)}, device_id_type=MESH
         )
+
+    @pl.when(active)
+    def _():
+        lane = lax.broadcasted_iota(jnp.int32, (CSLOT, HSIZE), 1)
+        row = lax.broadcasted_iota(jnp.int32, (CSLOT, HSIZE), 0)
+
+        @pl.loop(0, sections * rows // CSLOT)
+        def _(group):
+            padded = jnp.logical_and(row >= group_len_of(group), lane == 0)
+            bias[aligned(group * CSLOT, CSLOT, CSLOT)] = jnp.where(padded, NEG_FILL, 0.0).astype(BF16)
+
+        ones[...] = jnp.where(
+            lax.broadcasted_iota(jnp.int32, ones.shape, 1) == 0, 1.0, 0.0
+        ).astype(BF16)
+
+        for block in range(blocks):
+            valid[block] = valid_rows(block)
+
     pl.semaphore_wait(barrier, sections - 1 + len(steps))
+
+    def tell(bit):
+        if bit < len(steps):
+            pl.semaphore_signal(
+                entered.at[bit], inc=1, device_id={"tensor": jnp.bitwise_xor(me_t, steps[bit])}, device_id_type=MESH
+            )
+
+    def hear(bit):
+        if bit < len(steps):
+            pl.semaphore_wait(entered.at[bit], 1)
+            tell(bit + 1)
+
+    tell(0)
 
     def send_kind(kind):
         @pl.loop(0, heads)
         def _(step):
-            index = lax.rem(step + me_s // 2, heads)
+            index = lax.rem(step + (me_s >> 1), heads)
             chip = chip_of(index, me_t, chips)
             for half_step in range(2):
                 target_core = core if half_step == 0 else 1 - core
@@ -165,33 +256,13 @@
     wait_sent(0)
     send_kind(2)
 
-    def group_len_of(group):
-        return len_ref[group]
-
-    for bit, step in enumerate(steps):
-        pl.semaphore_signal(
-            entered.at[bit], inc=1, device_id={"tensor": jnp.bitwise_xor(me_t, step)}, device_id_type=MESH
-        )
-        pl.semaphore_wait(entered.at[bit], 1)
-
     to_itself = me_t < half_tensors
 
     @pl.when(active)
     def _():
-        lane = lax.broadcasted_iota(jnp.int32, (CSLOT, HSIZE), 1)
-        row = lax.broadcasted_iota(jnp.int32, (CSLOT, HSIZE), 0)
-
-        @pl.loop(0, sections * rows // CSLOT)
-        def _(group):
-            padded = jnp.logical_and(row >= group_len_of(group), lane == 0)
-            bias[aligned(group * CSLOT, CSLOT, CSLOT)] = jnp.where(padded, NEG_FILL, 0.0).astype(BF16)
-
-        ones[...] = jnp.where(
-            lax.broadcasted_iota(jnp.int32, ones.shape, 1) == 0, 1.0, 0.0
-        ).astype(BF16)
-
         forward(0)
 
+    hear(0)
     wait_sent(1)
     send_kind(3)
 
@@ -202,56 +273,6 @@
             wait_arrival(1, section)
 
         wait_forwarded(0)
-
-        def p_span(block, index, count=1):
-            return pl.ds((block * (block + 1) // 2 + index) * key_rows, count * key_rows)
-
-        def key_span(index, count=1):
-            return pl.ds(index * key_rows, count * key_rows)
-
-        def own_span(block):
-            return pl.ds(block * rows, rows)
-
-        lane_q = lax.broadcasted_iota(jnp.int32, (1, rows), 1)
-        query_place = jnp.where(
-            lane_q < half_rows, core * half_rows + lane_q, rows + (1 - core) * half_rows + lane_q - half_rows
-        )
-
-        def send_out(block, first, last, group):
-            column = aligned((me_t * heads + head) * HSIZE, HSIZE, HSIZE)
-            for unit in range(2):
-                section = 2 * block + unit
-
-                @pl.loop(0, half_rows // chunk)
-                def _(index):
-                    tensor = half_of(unit, core) * half_tensors + index
-                    start = block * rows + unit * half_rows + index * chunk
-                    source = stage.at[pl.ds(first, last - first), aligned(start, chunk, chunk)]
-                    place = out_ref.at[pl.ds(first, last - first), :, column]
-                    itself = jnp.logical_and(section == me_s, tensor == me_t)
-
-                    @pl.when(jnp.logical_not(itself))
-                    def _():
-                        pltpu.make_async_remote_copy(
-                            src_ref=source, dst_ref=place,
-                            send_sem=osend_sem.at[group], recv_sem=orecv_sem.at[group],
-                            device_id={"section": section, "tensor": tensor}, device_id_type=MESH,
-                        ).start()
-
-                    @pl.when(itself)
-                    def _():
-                        pltpu.make_async_copy(source, place, orecv_sem.at[group]).start()
-
-        def valid_rows(block):
-            piece = lane_q // CSLOT
-            length = jnp.zeros((1, rows), jnp.int32)
-            for unit in range(2):
-                first = ((2 * block + unit) * rows + half_of(unit, core) * half_rows) // CSLOT
-                for inner in range(half_rows // CSLOT):
-                    length = jnp.where(
-                        piece == unit * (half_rows // CSLOT) + inner, group_len_of(first + inner), length
-                    )
-            return lax.rem(lane_q, CSLOT) < length
 
         for block in range(blocks):
             span = key_span(block)
@@ -271,6 +292,11 @@
             tops[block] = top
 
         forward(2)
+
+    hear(1)
+
+    @pl.when(active)
+    def _():
         wait_forwarded(2)
 
         for block in range(blocks):
@@ -284,13 +310,13 @@
             totals[block] = total
             out_t = dot(vt[:, key_span(0, block + 1)], low, (1, 0))
             outt[block] = out_t
-            keep = jnp.where(valid_rows(block), 1.0 / total, 0.0)
-            stage[0, own_span(block)] = (out_t * keep).T.astype(BF16)
-            send_out(block, 0, 1, 0)
-
-        @pl.loop(0, sections)
-        def _(section):
-            wait_arrival(3, section)
+            stage[0, own_span(block)] = (out_t * (valid[block] / total)).astype(BF16).T
+
+    hear(2)
+
+    @pl.when(active)
+    def _():
+        send_out(0, 1, 0)
 
         def finish(block):
             pltpu.make_async_copy(xrecv.at[block], xrecv.at[block], xrecv_sem.at[block]).wait()
@@ -300,17 +326,30 @@
                 part = pl.ds(unit * half_rows, half_rows)
                 stage[2, to] = ((dk[mine] + xrecv[block, 0, part].astype(F32)) * score_scale).astype(BF16)
                 stage[3, to] = (dv[mine] + xrecv[block, 1, part].astype(F32)).astype(BF16)
-            send_out(block, 1, 4, 1)
-
-        for block in reversed(range(blocks)):
+
+        def exchange(block):
+            for unit in range(2):
+                theirs = key_rows_of(2 * block + unit, half_of(unit, 1 - core))
+                part = pl.ds(unit * half_rows, half_rows)
+                xsend[block, 0, part] = dk[theirs].astype(BF16)
+                xsend[block, 1, part] = dv[theirs].astype(BF16)
+            pltpu.make_async_remote_copy(
+                src_ref=xsend.at[block], dst_ref=xrecv.at[block],
+                send_sem=xsend_sem, recv_sem=xrecv_sem.at[block],
+                device_id={"section": sibling}, device_id_type=MESH,
+            ).start()
+
+        done, waiting, exchanged = [], list(reversed(range(blocks))), []
+        for block in list(range(blocks - 1, -1, -2)) + list(range(blocks - 2, -1, -2)):
             own = own_span(block)
             inverse = 1.0 / totals[block]
-            keep = jnp.where(valid_rows(block), inverse, 0.0)
-            grad_t = gbuf[own].T.astype(F32) * keep
+            wait_arrival(3, 2 * block)
+            wait_arrival(3, 2 * block + 1)
+            grad_t = gbuf[own].T.astype(F32) * (valid[block] * inverse)
             out_t = outt[block]
             delta = jnp.sum(grad_t * out_t, axis=0, keepdims=True) * inverse
             grad_low_t = grad_t.astype(BF16)
-            grad_low = grad_t.T.astype(BF16)
+            grad_low = grad_low_t.T
             query_now = qbuf[own]
             dq_t = jnp.zeros((HSIZE, rows), F32)
             for index in range(0, block + 1, 2):
@@ -324,22 +363,20 @@
                 dv[span] = dv_part if block == blocks - 1 else dv[span] + dv_part
                 dk[span] = dk_part if block == blocks - 1 else dk[span] + dk_part
                 dq_t += dot(kt[:, span], score_grad, (1, 0))
-            stage[1, own] = (dq_t * score_scale).T.astype(BF16)
-            for unit in range(2):
-                theirs = key_rows_of(2 * block + unit, half_of(unit, 1 - core))
-                part = pl.ds(unit * half_rows, half_rows)
-                xsend[block, 0, part] = dk[theirs].astype(BF16)
-                xsend[block, 1, part] = dv[theirs].astype(BF16)
-            pltpu.make_async_remote_copy(
-                src_ref=xsend.at[block], dst_ref=xrecv.at[block],
-                send_sem=xsend_sem, recv_sem=xrecv_sem.at[block],
-                device_id={"section": sibling}, device_id_type=MESH,
-            ).start()
-
-            if block < blocks - 1:
-                finish(block + 1)
-
-        finish(0)
+            stage[1, own] = (dq_t * score_scale).astype(BF16).T
+            send_out(1, 2, 1, block)
+            for other in exchanged:
+                finish(other)
+            done.append(block)
+            exchanged = [other for other in waiting if all(later in done for later in range(other, blocks))]
+            for other in exchanged:
+                waiting.remove(other)
+                exchange(other)
+
+        for other in exchanged:
+            finish(other)
+
+        send_out(2, 4, 2)
 
         for kind in (0, 2):
             part = landing[kind].at[pl.ds(0, sections * half_rows)]
@@ -347,7 +384,7 @@
         pltpu.make_async_copy(xsend, xsend, xsend_sem).wait()
 
         own_rows = sections * half_rows
-        for group, (first, last) in enumerate(((0, 1), (1, 4))):
+        for group, (first, last) in enumerate(((0, 1), (1, 2), (2, 4))):
             @pl.when(to_itself)
             def _():
                 part = stage.at[pl.ds(first, last - first), pl.ds(0, own_rows - chunk)]
@@ -360,7 +397,7 @@
 
     wait_sent(2)
     wait_sent(3)
-    for group, (first, last) in enumerate(((0, 1), (1, 4))):
+    for group, (first, last) in enumerate(((0, 1), (1, 2), (2, 4))):
         part = out_ref.at[pl.ds(first, last - first)]
         pltpu.make_async_copy(part, part, orecv_sem.at[group]).wait()
 
@@ -396,6 +433,7 @@
             vmem((blocks, HSIZE, rows), F32),
             vmem((blocks, 8, rows), F32),
             vmem((blocks, 1, rows), F32),
+            vmem((blocks, 1, rows), F32),
             vmem((seq_len, HSIZE), F32),
             vmem((seq_len, HSIZE), F32),
             vmem((4, own, HSIZE), BF16),
@@ -407,8 +445,8 @@
             dma((2,)),
             dma,
             dma((blocks,)),
-            dma((2,)),
-            dma((2,)),
+            dma((3,)),
+            dma((3,)),
             pltpu.SemaphoreType.REGULAR((tensors.bit_length() - 1,)),
         ],
         compiler_params=pltpu.CompilerParams(

time: 76.3 us -> 73.8 us (0.967)
  Pallas kernels: 73 us -> 70.5 us
    pallas_call x1, Pallas kernels: 73 us -> 70.5 us  [per_device(): pl.pallas_call(functools.partial(attention_kernel, sections, tensors, hea...]
where the time goes in v4:
time: 73.8 us; the launch traced here: 73.7 us
  Pallas kernels  70.5 us (96%)
  local copies, waits for them, and re-layouts  2.51 us (3%)
    pallas_call x1, Pallas kernels, per_device(): pl.pallas_call(functools.partial(attention_kernel, sections, tensors, hea...  70.5 us
    squeeze x1, local copies, waits for them, and re-layouts, per_device(): return tuple((out[index] for index in range(4)))  2.51 us

profile of v4, /device:TPU:1, one launch (start us, length us, event | category | flops | bytes accessed | tf_op | source)
XLA Modules:
  0.0 73.7 jit_solution(647693334188597272)
XLA Ops:
  0.6 70.5 %shard_map.84 = bf16[4,32,6144]{2,1,0:T(8,128)(2,1)} custom-call(s32[64]{0:T(128)} %len_ref.1, bf16[256,768]{1,0:T(8,128)(2,1)} %q_ref.1, bf16[256,768]{1,0:T(8,128)(2,1)} %k_ref.1, bf16[256,768]{1,0:T(8,128)(2,1)} %v_ref.1, bf16[256,768]{1,0:T(8,128)(2,1)} %g_ref.1), custom_call_target="tpu_custom_call" | custom-call | flops 6442450944 | bytes 3145728 | tf_op jit(solution)/shard_map/pallas_call | solution.py:417
  71.2 2.5 %slice_bitcast_fusion = (bf16[32,6144]{1,0:T(8,128)(2,1)}, bf16[32,6144]{1,0:T(8,128)(2,1)}, bf16[32,6144]{1,0:T(8,128)(2,1)}, bf16[32,6144]{1,0:T(8,128)(2,1)}) fusion(bf16[4,32,6144]{2,1,0:T(8,128)(2,1)} %shard_map.84), kind=kLoop, calls=%fused_computation | loop fusion | bytes 3145728 | tf_op jit(solution)/shard_map/squeeze | solution.py:461

commit v5 on v4

--- a/solution.py
+++ b/solution.py
@@ -16,11 +16,11 @@
 BF16 = jnp.bfloat16
 
 
-def chip_of(head, tensor, chips):
+def chip_at(chip, step, chips):
     if chips != 8:
-        return lax.rem(head + tensor, chips)
-    level = (head >= 3).astype(jnp.int32)
-    return 2 * (head - level + (tensor >> 1) & 3) + level
+        return lax.rem(chip + step + 1, chips)
+    dx, dz = ((2, 1), (2, 0), (1, 1), (3, 1), (1, 0), (3, 0), (0, 1), (0, 0))[step]
+    return 2 * ((chip >> 1) + dx & 3) + (chip + dz & 1)
 
 
 def section_at(section, step, sections):
@@ -183,37 +183,30 @@
 
     tell(0)
 
+    turns = []
+    for step in range(chips):
+        chip = chip_at(me_s >> 1, step, chips)
+        turns.append((chip,) + head_at(chip, me_t, chips, heads))
+
     def send_kind(kind):
-        @pl.loop(0, heads)
-        def _(step):
-            index = lax.rem(step + (me_s >> 1), heads)
-            chip = chip_of(index, me_t, chips)
-            for half_step in range(2):
-                target_core = core if half_step == 0 else 1 - core
-                target = 2 * chip + target_core
-                half = half_of(me_s, target_core)
-                source = inputs[kind].at[
-                    aligned(half * half_rows, half_rows, half_rows), aligned(index * HSIZE, HSIZE, HSIZE)
-                ]
-                place = slot(kind, me_s, half)
-
-                def send():
-                    pltpu.make_async_remote_copy(
-                        src_ref=source, dst_ref=place,
-                        send_sem=send_sem.at[kind], recv_sem=recv_sem.at[kind, me_s],
-                        device_id={"section": target}, device_id_type=MESH,
-                    ).start()
-
-                if half_step == 0:
-                    @pl.when(target != me_s)
-                    def _():
-                        send()
-
-                    @pl.when(target == me_s)
-                    def _():
+        for step, (chip, index, busy) in enumerate(turns):
+            @pl.when(busy)
+            def _():
+                for half_step in range(2):
+                    target_core = core if half_step == 0 else 1 - core
+                    half = half_of(me_s, target_core)
+                    source = inputs[kind].at[
+                        aligned(half * half_rows, half_rows, half_rows), aligned(index * HSIZE, HSIZE, HSIZE)
+                    ]
+                    place = slot(kind, me_s, half)
+                    if step == chips - 1 and half_step == 0:
                         pltpu.make_async_copy(source, place, recv_sem.at[kind, me_s]).start()
-                else:
-                    send()
+                    else:
+                        pltpu.make_async_remote_copy(
+                            src_ref=source, dst_ref=place,
+                            send_sem=send_sem.at[kind], recv_sem=recv_sem.at[kind, me_s],
+                            device_id={"section": 2 * chip + target_core}, device_id_type=MESH,
+                        ).start()
 
     def wait_sent(kind):
         @pl.when(active)
@@ -400,6 +393,19 @@
     for group, (first, last) in enumerate(((0, 1), (1, 2), (2, 4))):
         part = out_ref.at[pl.ds(first, last - first)]
         pltpu.make_async_copy(part, part, orecv_sem.at[group]).wait()
+
+
+def split_kernel(out_ref, *refs):
+    *parts, held, in_sem, out_sem = refs
+    loads = [pltpu.make_async_copy(out_ref.at[index], held.at[index], in_sem.at[index]) for index in range(4)]
+    stores = [pltpu.make_async_copy(held.at[index], parts[index], out_sem.at[index]) for index in range(4)]
+    for load in loads:
+        load.start()
+    for load, store in zip(loads, stores):
+        load.wait()
+        store.start()
+    for store in stores:
+        store.wait()
 
 
 def per_device(query_in, key_in, value_in, out_grad, group_len):
@@ -458,7 +464,13 @@
             transcendentals=seq_len * seq_len // 4,
         ),
     )(group_len, query_in, key_in, value_in, out_grad)
-    return tuple(out[index] for index in range(4))
+    return pl.pallas_call(
+        split_kernel,
+        out_shape=[jax.ShapeDtypeStruct(out.shape[1:], BF16)] * 4,
+        in_specs=[anywhere],
+        out_specs=[anywhere] * 4,
+        scratch_shapes=[vmem(out.shape, BF16), dma((4,)), dma((4,))],
+    )(out)
 
 
 def solution(mesh):

time: 73.8 us -> 73 us (0.989)
  local copies, waits for them, and re-layouts: 2.51 us -> 0 us
  Pallas kernels: 70.5 us -> 71.8 us
    squeeze x1 -> x0, local copies, waits for them, and re-layouts: 2.51 us -> none  [per_device(): return tuple((out[index] for index in range(4)))]
    pallas_call x0 -> x1, Pallas kernels: none -> 2.2 us  [per_device(): pl.pallas_call(split_kernel, out_shape=[jax.ShapeDtypeStruct(out.shape[1:...]
    pallas_call x1, Pallas kernels: 70.5 us -> 69.6 us  [per_device(): pl.pallas_call(functools.partial(attention_kernel, sections, tensors, hea...]
where the time goes in v5:
time: 73 us; the launch traced here: 72.6 us
  Pallas kernels  71.8 us (98%)
  between operations  0.8 us (1%)
    pallas_call x1, Pallas kernels, per_device(): pl.pallas_call(functools.partial(attention_kernel, sections, tensors, hea...  69.6 us
    pallas_call x1, Pallas kernels, per_device(): pl.pallas_call(split_kernel, out_shape=[jax.ShapeDtypeStruct(out.shape[1:...  2.2 us

profile of v5, /device:TPU:1, one launch (start us, length us, event | category | flops | bytes accessed | tf_op | source)
XLA Modules:
  0.0 72.6 jit_solution(7104057512230546687)
XLA Ops:
  0.6 69.6 %shard_map.84.out_ref = bf16[4,32,6144]{2,1,0:T(8,128)(2,1)} custom-call(s32[64]{0:T(128)} %len_ref.1, bf16[256,768]{1,0:T(8,128)(2,1)} %q_ref.1, bf16[256,768]{1,0:T(8,128)(2,1)} %k_ref.1, bf16[256,768]{1,0:T(8,128)(2,1)} %v_ref.1, bf16[256,768]{1,0:T(8,128)(2,1)} %g_ref.1), custom_call_target="tpu_custom_call" | custom-call | flops 6442450944 | bytes 3145728 | tf_op jit(solution)/shard_map/pallas_call | solution.py:423
  70.2 2.2 %shard_map.85 = (bf16[32,6144]{1,0:T(8,128)(2,1)}, bf16[32,6144]{1,0:T(8,128)(2,1)}, bf16[32,6144]{1,0:T(8,128)(2,1)}, bf16[32,6144]{1,0:T(8,128)(2,1)}) custom-call(bf16[4,32,6144]{2,1,0:T(8,128)(2,1)} %shard_map.84.out_ref), custom_call_target="tpu_custom_call" | custom-call | tf_op jit(solution)/shard_map/pallas_call | solution.py:467

commit v6 on v5

--- a/solution.py
+++ b/solution.py
@@ -356,15 +356,16 @@
                 dv[span] = dv_part if block == blocks - 1 else dv[span] + dv_part
                 dk[span] = dk_part if block == blocks - 1 else dk[span] + dk_part
                 dq_t += dot(kt[:, span], score_grad, (1, 0))
+            done.append(block)
+            ready = [other for other in waiting if all(later in done for later in range(other, blocks))]
+            for other in ready:
+                waiting.remove(other)
+                exchange(other)
             stage[1, own] = (dq_t * score_scale).astype(BF16).T
             send_out(1, 2, 1, block)
             for other in exchanged:
                 finish(other)
-            done.append(block)
-            exchanged = [other for other in waiting if all(later in done for later in range(other, blocks))]
-            for other in exchanged:
-                waiting.remove(other)
-                exchange(other)
+            exchanged = ready
 
         for other in exchanged:
             finish(other)

time: 73 us -> 72.3 us (level)
  no operation moved by 1% of the time
where the time goes in v6:
time: 72.3 us; the launch traced here: 71.9 us
  Pallas kernels  71.1 us (98%)
  between operations  0.8 us (1%)
    pallas_call x1, Pallas kernels, per_device(): pl.pallas_call(functools.partial(attention_kernel, sections, tensors, hea...  68.9 us
    pallas_call x1, Pallas kernels, per_device(): pl.pallas_call(split_kernel, out_shape=[jax.ShapeDtypeStruct(out.shape[1:...  2.2 us

profile of v6, /device:TPU:1, one launch (start us, length us, event | category | flops | bytes accessed | tf_op | source)
XLA Modules:
  0.0 71.9 jit_solution(1881029326893525569)
XLA Ops:
  0.6 68.9 %shard_map.84.out_ref = bf16[4,32,6144]{2,1,0:T(8,128)(2,1)} custom-call(s32[64]{0:T(128)} %len_ref.1, bf16[256,768]{1,0:T(8,128)(2,1)} %q_ref.1, bf16[256,768]{1,0:T(8,128)(2,1)} %k_ref.1, bf16[256,768]{1,0:T(8,128)(2,1)} %v_ref.1, bf16[256,768]{1,0:T(8,128)(2,1)} %g_ref.1), custom_call_target="tpu_custom_call" | custom-call | flops 6442450944 | bytes 3145728 | tf_op jit(solution)/shard_map/pallas_call | solution.py:424
  69.5 2.2 %shard_map.85 = (bf16[32,6144]{1,0:T(8,128)(2,1)}, bf16[32,6144]{1,0:T(8,128)(2,1)}, bf16[32,6144]{1,0:T(8,128)(2,1)}, bf16[32,6144]{1,0:T(8,128)(2,1)}) custom-call(bf16[4,32,6144]{2,1,0:T(8,128)(2,1)} %shard_map.84.out_ref), custom_call_target="tpu_custom_call" | custom-call | tf_op jit(solution)/shard_map/pallas_call | solution.py:468
